TPU v7x, 32 devices: a whole 2x2x4 slice. The times are simulated.
32 devices in a mesh: groups: 2 (over x), particle: 8 (over z, y), seq: 2 (over core).
Axes of the slice: x: 2, y: 2, z: 4, core: 2. Of those that a mesh axis runs over, the one named last changes fastest.
Arguments:
- latents: float32 [16, 1024, 64], P(('groups', 'particle'), 'seq'), parts along dimension 0, may hold values from -6 to 6
- text_kv: bfloat16 [16, 2, 256, 1536], P(('groups', 'particle'), None, None, 'seq'), parts along dimension 0, may hold values from -20 to 20
- ancestors: int32 [16], P('groups'), parts along dimension 0, may hold values from 0 to 7
- order: int32 [16], P('groups'), parts along dimension 0, may hold values from 0 to 7, each once
- embed_weight: bfloat16 [64, 3072], replicated, may hold values from -0.75 to 0.75
- embed_bias: float32 [3072], replicated, may hold values from -3 to 3
- shift: float32 [6144], P('groups'), parts along dimension 0, may hold values from -3 to 3
- scale: float32 [6144], P('groups'), parts along dimension 0, may hold values from -0.9 to 0.9
- qkv_weight: bfloat16 [3072, 4608], P(None, 'seq'), may hold values from -4 to 4
- norm_gains: float32 [2, 128], replicated, may hold values from 0.5 to 2
Outputs:
- attended: bfloat16 [16, 1024, 1536], P(('groups', 'particle'), 'seq'), parts along dimension 0
There are 2 independent parts, one for each index of `groups`. A program takes and returns all parts, laid end to end along the dimension named above; an argument that names none is the same for every part. Nothing has to cross between parts.
All inputs are finite; a program needn't handle non-finite values.
Results may differ from a plain program's by a relative error of at most 0.012.
The roundings to bfloat16 on the way count: a program that leaves them out, or rounds other values in their place, can miss the bound.
Values may be sent and summed in bfloat16 or wider, within the bound.
A program may use at most 128 MiB of HBM per device.

v0:
```python
import jax
import jax.numpy as jnp
from jax import lax
from jax.sharding import PartitionSpec as P


def rms_norm(values, gain):
    return values * lax.rsqrt(jnp.mean(values * values, axis=-1, keepdims=True) + 1e-06) * gain


def embed_rows(lat_rows, embed_weight, embed_bias, shift, scale):
    embedded = (
        jnp.einsum("prc,cd->prd", lat_rows, embed_weight, preferred_element_type=jnp.float32)
        + embed_bias
    )
    center = embedded - jnp.mean(embedded, axis=-1, keepdims=True)
    spread = jnp.mean(center * center, axis=-1, keepdims=True)
    return (center * lax.rsqrt(spread + 1e-06) * (1.0 + scale) + shift).astype(jnp.bfloat16)


def project_rows(normed, qkv_weight, norm_gains):
    width = norm_gains.shape[1]
    local_heads = qkv_weight.shape[1] // (3 * width)
    mixed = jnp.einsum("prd,dc->prc", normed, qkv_weight, preferred_element_type=jnp.float32)
    mixed = mixed.reshape(normed.shape[0], normed.shape[1], local_heads, 3, width)
    query = rms_norm(mixed[:, :, :, 0], norm_gains[0])
    key_img = rms_norm(mixed[:, :, :, 1], norm_gains[1])
    stacked = jnp.stack([query, key_img, mixed[:, :, :, 2]], axis=3)
    return stacked.reshape(normed.shape[0], normed.shape[1], local_heads * 3 * width).astype(
        jnp.bfloat16
    )


def body(
    latents,
    text_kv,
    ancestors,
    order,
    embed_weight,
    embed_bias,
    shift,
    scale,
    qkv_weight,
    norm_gains,
):
    p_dev = latents.shape[0]
    width = norm_gains.shape[1]
    local_heads = qkv_weight.shape[1] // (3 * width)
    chosen = ancestors[order]
    lat_half = latents.astype(jnp.bfloat16)
    every_lat, every_kv = (
        lax.all_gather(lat_half, "particle", axis=0, tiled=True),
        lax.all_gather(text_kv, "particle", axis=0, tiled=True),
    )
    mine = lax.axis_index("particle") * p_dev + jnp.arange(p_dev, dtype=jnp.int32)
    source = chosen[mine]
    new_lat = jnp.take(every_lat, source, axis=0)
    new_kv = jnp.take(every_kv, source, axis=0)
    normed = embed_rows(new_lat, embed_weight, embed_bias, shift, scale)
    packed = project_rows(lax.all_gather(normed, "seq", axis=1, tiled=True), qkv_weight, norm_gains)
    tokens = packed.shape[1]
    packed = packed.reshape(p_dev, tokens, local_heads, 3, width)
    text_len = new_kv.shape[2]
    text_keys = new_kv[:, 0].reshape(p_dev, text_len, local_heads, width)
    text_vals = new_kv[:, 1].reshape(p_dev, text_len, local_heads, width)
    keys = jnp.concatenate([text_keys, packed[:, :, :, 1]], axis=1)
    vals = jnp.concatenate([text_vals, packed[:, :, :, 2]], axis=1)
    scores = jnp.einsum(
        "pqhd,pkhd->phqk", packed[:, :, :, 0], keys, preferred_element_type=jnp.float32
    )
    scores = scores / jnp.sqrt(jnp.float32(width))
    weights = jax.nn.softmax(scores, axis=-1).astype(jnp.bfloat16)
    output = jnp.einsum("phqk,pkhd->pqhd", weights, vals, preferred_element_type=jnp.float32)
    output = output.reshape(p_dev, tokens, local_heads * width).astype(jnp.bfloat16)
    return lax.all_to_all(output, "seq", split_axis=1, concat_axis=2, tiled=True)


def solution(mesh):
    in_specs = (
        P(("groups", "particle"), "seq", None),
        P(("groups", "particle"), None, None, "seq"),
        P("groups"),
        P("groups"),
        P(),
        P(),
        P("groups"),
        P("groups"),
        P(None, "seq"),
        P(),
    )
    out_specs = P(("groups", "particle"), "seq", None)
    return jax.shard_map(body, mesh=mesh, in_specs=in_specs, out_specs=out_specs, check_vma=False)
```

profile of v0, /device:TPU:1, one launch (start us, length us, event | category | flops | bytes accessed | tf_op | source)
XLA Modules:
  0.0 244.0 jit_solution(4653902274258375800)
XLA Ops:
  6.5 0.7 compare_select_fusion
  7.3 1.3 gather_fusion
  8.6 0.6 dynamic-slice.8
  11.0 0.9 convert_element_type.43
  11.9 26.9 %all_gather.10 = bf16[8,512,64]{1,2,0:T(8,128)(2,1)S(1)} all-gather(bf16[1,512,64]{1,2,0:T(8,128)(2,1)S(1)} %convert_element_type.43), channel_id=1, replica_groups=mesh['groups'=2,'particle'=8,'seq'=2] {'particle'}, dimensions={0}, use_global_device_ids=true | all-gather | bytes 589824 | tf_op jit(solution)/shard_map/all_gather | solution.py:52
  38.9 1.9 add_reduce_fusion
  40.8 0.9 multiply_reduce_fusion.1
  41.8 3.4 %add_convert_fusion = bf16[512,3072]{1,0:T(8,128)(2,1)} fusion(f32[512,3072]{1,0:T(8,128)S(1)} %get-tuple-element.47, f32[3072]{0:T(1024)S(1)} %copy-done.6, f32[3072]{0:T(1024)S(1)} %broadcast_add_fusion, f32[512]{0:T(512)S(1)} %add_rsqrt_fusion.2, f32[512]{0:T(512)S(1)} %broadcast_multiply_fusion, f32[3072]{0:T(1024)S(1)} %copy-done.4), kind=kLoop, calls=%fused_computation.11 | loop fusion | flops 9437184 | bytes 9478144 | tf_op jit(solution)/shard_map/convert_element_type | solution.py:18
  45.2 0.2 all-gather.4.cloned.1.call-start
  45.4 0.5 all-gather.4.cloned.1.call-update
  46.0 19.0 %copy.34 = bf16[3072,2304]{0,1:T(8,128)(2,1)} copy(bf16[3072,2304]{1,0:T(8,128)(2,1)} %param.18) | data formatting | bytes 28311552 | tf_op args[8]
  65.0 4.1 %all-gather.6.cloned.1.call-done = bf16[1024,3072]{1,0:T(8,128)(2,1)} async-done(((bf16[512,3072]{1,0:T(8,128)(2,1)}), bf16[1024,3072]{1,0:T(8,128)(2,1)}) %all-gather.6.cloned.1.call-update) | async-done | bytes 6291472 | tf_op jit(solution)/shard_map/all_gather | solution.py:60
  69.1 19.8 %fusion.10 = f32[1,1024,6,3,128]{4,1,3,2,0:T(8,128)S(1)} fusion(bf16[6,3,128,3072]{3,2,1,0:T(8,128)(2,1)} %bitcast.71, bf16[1024,3072]{1,0:T(8,128)(2,1)} %all-gather.6.cloned.1.call-done), kind=kOutput, calls=%fused_computation.14 | convolution fusion | flops 14495514624 | bytes 29884416 | tf_op jit(solution)/shard_map/prd,dc->prc/dot_general | solution.py:24
  88.8 1.7 multiply_reduce_fusion.2
  90.6 1.4 fusion.30
  91.9 2.9 %fusion.29 = (bf16[1,1024,6,128]{3,1,2,0:T(8,128)(2,1)S(1)}, bf16[1024,6,128]{2,0,1:T(8,128)(2,1)}) fusion(f32[1,1024,6,3,128]{4,1,3,2,0:T(8,128)S(1)} %fusion.10, f32[128]{0:T(128)S(1)} %get-tuple-element.44, f32[1024,6]{0,1:T(8,128)S(1)} %get-tuple-element.48, f32[128]{0:T(128)S(1)} %get-tuple-element.45, f32[1024,6]{0,1:T(8,128)S(1)} %get-tuple-element.49), kind=kLoop, calls=%fused_computation.26 | loop fusion | flops 4718592 | bytes 9487360 | tf_op jit(solution)/shard_map/squeeze | solution.py:66
  94.9 75.7 %all-gather.4.cloned.1.call-done = bf16[8,2,256,768]{3,2,1,0:T(8,128)(2,1)} async-done(((bf16[1,2,256,768]{3,2,1,0:T(8,128)(2,1)}), bf16[8,2,256,768]{3,2,1,0:T(8,128)(2,1)}) %all-gather.4.cloned.1.call-update) | async-done | bytes 6291472 | tf_op jit(solution)/shard_map/all_gather | solution.py:53
  170.6 1.2 constant_dynamic-slice_fusion
  171.8 0.3 copy.44
  172.2 0.9 copy.36
  173.2 0.9 copy.35
  174.1 11.2 %fusion.51 = f32[6,1024]{1,0:T(8,128)} fusion(bf16[1024,6,128]{2,0,1:T(8,128)(2,1)} %get-tuple-element.41, bf16[1,1024,6,128]{3,1,2,0:T(8,128)(2,1)S(1)} %get-tuple-element.40, bf16[1,256,6,128]{3,1,2,0:T(8,128)(2,1)} %copy.36), kind=kOutput, calls=%fused_computation.54 | convolution fusion | flops 2040792320 | bytes 3563520 | tf_op jit(solution)/shard_map/sub | solution.py:72
  185.2 17.0 %fusion.23 = bf16[6,128,1024]{2,1,0:T(8,128)(2,1)} fusion(f32[6,1024]{1,0:T(8,128)} %fusion.51, bf16[1024,6,128]{2,0,1:T(8,128)(2,1)} %get-tuple-element.41, bf16[1,1024,6,128]{3,1,2,0:T(8,128)(2,1)S(1)} %copy-done.2, bf16[1,256,6,128]{3,1,2,0:T(8,128)(2,1)} %copy.35, bf16[1,1024,6,128]{3,1,2,0:T(8,128)(2,1)S(1)} %get-tuple-element.40, ...), kind=kOutput, calls=%fused_computation.24 | convolution fusion | flops 4066647296 | bytes 7102464 | tf_op jit(solution)/shard_map/phqk,pkhd->pqhd/dot_general | solution.py:73
  202.2 7.5 %copy.38 = bf16[1,1024,768]{2,0,1:T(2,128)(2,1)S(1)} copy(bf16[1,1024,768]{1,2,0:T(8,128)(2,1)} %bitcast.78) | data formatting | bytes 3145728 | tf_op jit(solution)/shard_map/convert_element_type | solution.py:74
  209.7 0.6 broadcast.178
  210.3 11.4 %reduce.12 = bf16[1024,768]{1,0:T(8,128)(2,1)} reduce(bf16[1024,1,768]{2,1,0:T(2,128)(2,1)S(1)} %bitcast.72, bf16[]{:T(256)} %broadcast.178), dimensions={1}, to_apply=%bitcast.57.reduce_sub_computation | reduce | bytes 3145730
  221.7 1.6 reshape.303
  223.3 6.6 %all_to_all.18 = bf16[2,2,196608]{2,1,0:T(2,128)(2,1)} all-to-all(bf16[2,2,196608]{2,1,0:T(2,128)(2,1)S(1)} %reshape.303), channel_id=1, replica_groups=mesh['groups'=2,'particle'=8,'seq'=2] {'seq'}, dimensions={0} | all-to-all | bytes 3145728 | tf_op jit(solution)/shard_map/all_to_all | solution.py:75
  229.9 2.5 %reshape.304 = bf16[1024,1,768]{2,1,0:T(2,128)(2,1)S(1)} reshape(bf16[2,2,196608]{2,1,0:T(2,128)(2,1)} %all_to_all.18) | data formatting | bytes 3145728
  232.4 1.4 copy.43
  233.8 1.7 copy.39
  235.6 1.6 copy.40
  (26 shorter events, 0.2 us)
Async XLA Ops:
  6.5 32.3 %copy-start = (bf16[64,3072]{1,0:T(8,128)(2,1)S(1)}, bf16[64,3072]{1,0:T(8,128)(2,1)}, u32[]{:S(2)}) copy-start(bf16[64,3072]{1,0:T(8,128)(2,1)} %param.14) | copy-start | bytes 1179652
  6.5 62.5 %all-gather.6.cloned.1.call-start = ((), (), s32[]{:S(2)}) async-start(), calls=%async_computation.2 | async-start | bytes 9437184 | tf_op jit(solution)/shard_map/all_gather | solution.py:60
  38.9 1.9 copy-start.4
  40.7 1.0 copy-start.5
  40.8 1.0 copy-start.6
  45.2 125.4 %all-gather.4.cloned.1.call-start = ((), (), s32[]{:S(2)}) async-start(), calls=%async_computation.1 | async-start | bytes 7077888 | tf_op jit(solution)/shard_map/all_gather | solution.py:53
  46.0 19.0 %copy-start.7 = (f32[2,128]{1,0:T(2,128)S(1)}, f32[2,128]{1,0:T(2,128)}, u32[]{:S(2)}) copy-start(f32[2,128]{1,0:T(2,128)} %param.19) | copy-start | bytes 3076
  174.1 11.2 %copy-start.2 = (bf16[1,1024,6,128]{3,1,2,0:T(8,128)(2,1)S(1)}, bf16[1,1024,6,128]{3,1,2,0:T(8,128)(2,1)}, u32[]{:S(2)}) copy-start(bf16[1,1024,6,128]{3,1,2,0:T(8,128)(2,1)} %fusion.30) | copy-start | bytes 4718596
  174.1 11.2 %copy-start.3 = (bf16[1,256,6,128]{3,1,2,0:T(8,128)(2,1)S(1)}, bf16[1,256,6,128]{3,1,2,0:T(8,128)(2,1)}, u32[]{:S(2)}) copy-start(bf16[1,256,6,128]{3,1,2,0:T(8,128)(2,1)} %copy.36) | copy-start | bytes 1179652
  232.4 4.7 %copy-start.1 = (bf16[64,3072]{1,0:T(8,128)(2,1)S(1)}, bf16[64,3072]{1,0:T(8,128)(2,1)}, u32[]{:S(2)}) copy-start(bf16[64,3072]{1,0:T(8,128)(2,1)} %param.14) | copy-start | bytes 1179652
Sparse Core Ops, SparseCore 0:
  45.3 23.6 all-gather.5
  71.2 99.3 all-gather.3
where the time goes:
time: 245 us; the launch traced here: 244 us
  waiting for transfers between devices  80.4 us (33%)
  matrix products  49.8 us (20%)
  local copies, waits for them, and re-layouts  42.4 us (17%)
  blocking collectives  33.6 us (14%)
  other arithmetic  22.2 us (9%)
  between operations  15.4 us (6%)
    all_gather x1, waiting for transfers between devices, body(): lax.all_gather(text_kv, 'particle', axis=0, tiled=True)  75.7 us
    all_gather x1, blocking collectives, body(): lax.all_gather(lat_half, 'particle', axis=0, tiled=True)  26.9 us
    unnamed x22, local copies, waits for them, and re-layouts  25.3 us
    dot_general x1, matrix products, project_rows(): jnp.einsum('prd,dc->prc', normed, qkv_weight, preferred_element_type=jnp....  19.8 us
    dot_general x1, matrix products, body(): jnp.einsum('phqk,pkhd->pqhd', weights, vals, preferred_element_type=jnp.f...  17 us
    unnamed x1, other arithmetic  11.4 us
    sub x1, matrix products, body(): weights = jax.nn.softmax(scores, axis=-1).astype(jnp.bfloat16)  11.2 us
    convert_element_type x1, local copies, waits for them, and re-layouts, body(): output.reshape(p_dev, tokens, local_heads * width).astype(jnp.bfloat16)  7.46 us
  transfers between devices with their start and end apart: 2, of which 2 were waited for; matrix products, arithmetic and copies ran while one was open for 18% of the time, Pallas kernels for 0%

commit v1 on v0

v1 whole, which is shorter than its diff:
```python
import functools
import jax
import jax.numpy as jnp
from jax import lax
from jax.experimental import pallas as pl
from jax.experimental.pallas import tpu as pltpu
from jax.sharding import PartitionSpec as P

LOG2E = 1.4426950408889634
BF16 = jnp.bfloat16
F32 = jnp.float32
NT = (((1,), (1,)), ((), ()))


def rms_norm(values, gain):
    return values * lax.rsqrt(jnp.mean(values * values, axis=-1, keepdims=True) + 1e-06) * gain


def project_kernel(x0_ref, x1_ref, ew_ref, eb_ref, sh_ref, sc_ref, gain_ref, w_ref,
                   q_ref, k_ref, v_ref, normed, *, chunk, width):
    half = x0_ref.shape[0] * 2
    lanes = x0_ref.shape[1] // 2

    @pl.when(pl.program_id(0) == 0)
    def _():
        for part, x_ref in enumerate((x0_ref, x1_ref)):
            for side in range(2):
                for at in range(0, half // 2, chunk):
                    x = x_ref[at:at + chunk, side * lanes:(side + 1) * lanes]
                    emb = jnp.dot(x, ew_ref[...], preferred_element_type=F32) + eb_ref[...]
                    center = emb - jnp.mean(emb, axis=-1, keepdims=True)
                    spread = jnp.mean(center * center, axis=-1, keepdims=True)
                    res = center * lax.rsqrt(spread + 1e-06) * (1.0 + sc_ref[...]) + sh_ref[...]
                    row = part * half + side * (half // 2) + at
                    normed[row:row + chunk, :] = res.astype(BF16)

    rows = normed.shape[0]
    heads = w_ref.shape[1] // (3 * width)
    step = 256

    @pl.loop(0, rows // step)
    def _(i):
        r = pl.ds(pl.multiple_of(i * step, step), step)
        mixed = jnp.dot(normed[r, :], w_ref[...], preferred_element_type=F32)
        for h in range(heads):
            c = slice(h * width, (h + 1) * width)
            base = h * 3 * width
            q_ref[r, c] = rms_norm(mixed[:, base:base + width], gain_ref[0:1, :]).astype(BF16)
            k_ref[r, c] = rms_norm(
                mixed[:, base + width:base + 2 * width], gain_ref[1:2, :]
            ).astype(BF16)
            v_ref[r, c] = mixed[:, base + 2 * width:base + 3 * width].astype(BF16)


def project(x0, x1, embed_weight, embed_bias, shift, scale, gains, weight):
    d, cols = weight.shape
    width = gains.shape[1]
    heads = cols // (3 * width)
    per = 2 if heads % 2 == 0 else 1
    rows = 4 * x0.shape[0]
    whole = lambda a: pl.BlockSpec(a.shape, lambda j: (0,) * a.ndim)
    small = (x0, x1, embed_weight, embed_bias[None], shift[None], scale[None], gains)
    out = jax.ShapeDtypeStruct((rows, heads * width), BF16)
    ospec = pl.BlockSpec((rows, per * width), lambda j: (0, j))
    return pl.pallas_call(
        functools.partial(project_kernel, chunk=min(128, x0.shape[0]), width=width),
        grid=(heads // per,),
        in_specs=[whole(a) for a in small]
        + [pl.BlockSpec((d, per * 3 * width), lambda j: (0, j))],
        out_specs=[ospec] * 3,
        out_shape=[out] * 3,
        scratch_shapes=[pltpu.VMEM((rows, d), BF16)],
        compiler_params=pltpu.CompilerParams(vmem_limit_bytes=44 * 1024 * 1024),
        cost_estimate=pl.CostEstimate(
            flops=2 * rows * d * cols, bytes_accessed=2 * d * cols + 6 * rows * heads * width,
            transcendentals=0),
        name="project",
    )(*small, weight)


def image_kernel(q_ref, k_ref, v_ref, acc_ref, sum_ref, *, chunk, unit):
    width = k_ref.shape[1]
    vals = jnp.concatenate([v_ref[...], jnp.ones_like(v_ref)], axis=1)
    for at in range(0, q_ref.shape[0], chunk):
        r = slice(at, at + chunk)
        s = lax.dot_general(q_ref[r, :], k_ref[...], NT, preferred_element_type=F32)
        p = jnp.exp2(s * unit).astype(BF16)
        o = jnp.dot(p, vals, preferred_element_type=F32)
        acc_ref[r, :] = o[:, :width]
        sum_ref[r, :] = o[:, width:]


def image_attention(q, k, v, half, width):
    tokens, cols = q.shape
    rows = tokens // 2
    heads = cols // width
    unit = LOG2E / width ** 0.5
    out = jax.ShapeDtypeStruct((rows, cols), F32)
    return pl.pallas_call(
        functools.partial(image_kernel, chunk=256, unit=unit),
        grid=(heads,),
        in_specs=[pl.BlockSpec((rows, width), lambda h: (half, h))]
        + [pl.BlockSpec((tokens, width), lambda h: (0, h))] * 2,
        out_specs=[pl.BlockSpec((rows, width), lambda h: (0, h))] * 2,
        out_shape=[out] * 2,
        compiler_params=pltpu.CompilerParams(vmem_limit_bytes=32 * 1024 * 1024),
        cost_estimate=pl.CostEstimate(
            flops=8 * rows * tokens * cols, bytes_accessed=6 * tokens * cols + 8 * rows * cols,
            transcendentals=rows * tokens * heads),
        name=f"image_{half}",
    )(q, k, v)


def text_kernel(q_ref, ka_ref, kb_ref, va_ref, vb_ref, acc_ref, sum_ref, out_ref, *, unit):
    width = ka_ref.shape[1]
    keys = jnp.concatenate([ka_ref[...], kb_ref[...]], axis=0)
    vals = jnp.concatenate([va_ref[...], vb_ref[...]], axis=0)
    vals = jnp.concatenate([vals, jnp.ones_like(vals)], axis=1)
    s = lax.dot_general(q_ref[...], keys, NT, preferred_element_type=F32) * unit
    top = jnp.maximum(jnp.max(s, axis=-1, keepdims=True), 0.0)
    p = jnp.exp2(s - top).astype(BF16)
    o = jnp.dot(p, vals, preferred_element_type=F32)
    fade = jnp.exp2(-top)
    total = sum_ref[...] * fade + o[:, width:]
    out_ref[...] = ((acc_ref[...] * fade + o[:, :width]) / total).astype(BF16)


def text_attention(q, ka, kb, va, vb, acc, total, half, width):
    tokens, cols = q.shape
    rows = tokens // 2
    heads = cols // width
    unit = LOG2E / width ** 0.5
    part = pl.BlockSpec((ka.shape[0], width), lambda h: (0, h))
    full = pl.BlockSpec((rows, width), lambda h: (0, h))
    return pl.pallas_call(
        functools.partial(text_kernel, unit=unit),
        grid=(heads,),
        in_specs=[pl.BlockSpec((rows, width), lambda h: (half, h))] + [part] * 4 + [full] * 2,
        out_specs=full,
        out_shape=jax.ShapeDtypeStruct((rows, cols), BF16),
        compiler_params=pltpu.CompilerParams(vmem_limit_bytes=32 * 1024 * 1024),
        cost_estimate=pl.CostEstimate(
            flops=16 * rows * ka.shape[0] * cols, bytes_accessed=14 * rows * cols,
            transcendentals=2 * rows * ka.shape[0] * heads),
        name=f"text_{half}",
    )(q, ka, kb, va, vb, acc, total)


def pack(lat):
    rows = lat.shape[0] // 2
    return jnp.concatenate([lat[:rows], lat[rows:]], axis=1)


def pick(which, choices):
    res = choices[0]
    for i, item in enumerate(choices[1:], 1):
        res = jnp.where(which == i, item, res)
    return res


def route_latents(lat, chosen, me):
    z, y = me // 2, me % 2
    held = [lat]
    for k in (1, 2, 3):
        held.append(lax.ppermute(
            lat, "particle", [(2 * a + b, 2 * ((a + k) % 4) + b) for a in range(4) for b in range(2)]))
    need = chosen[me]
    other = chosen[me ^ 1]
    mine = pick((z - need // 2) % 4, held)
    theirs = pick((z - other // 2) % 4, held)
    swap = [(p, p ^ 1) for p in range(8)]
    flip = [(0, 1), (1, 0)]
    diag = [(2 * p + s, 2 * (p ^ 1) + (1 - s)) for p in range(8) for s in range(2)]
    from_y = lax.ppermute(theirs, "particle", swap)
    from_seq = lax.ppermute(mine, "seq", flip)
    from_diag = lax.ppermute(theirs, ("particle", "seq"), diag)
    here = need % 2 == y
    return jnp.where(here, from_seq, from_diag), jnp.where(here, mine, from_y)


def route_text(kv, chosen, me, after):
    z, y = me // 2, me % 2
    swap = [(p, p ^ 1) for p in range(8)]
    middle = [(2, 4), (3, 5), (4, 2), (5, 3)]
    inward = [(0, 2), (1, 3), (6, 4), (7, 5)]
    beyond = [(0, 4), (1, 5), (6, 2), (7, 3)]
    outward = [(2, 0), (3, 1), (4, 6), (5, 7)]
    rows = kv.shape[1] // 2
    got = []
    plane = jnp.where(z < 2, 0, 3)
    planes = []
    for c in range(2):
        halves = kv[c].reshape(2, rows, kv.shape[2])
        own = jnp.where(y == 0, halves[0], halves[1])
        give = jnp.where(y == 0, halves[1], halves[0])
        recv = lax.ppermute(give, "particle", swap)
        planes.append(jnp.stack([jnp.where(y == 0, own, recv), jnp.where(y == 0, recv, own)]))
    planes, _ = lax.optimization_barrier((planes, after))
    for c in range(2):
        own = planes[c]
        held = [own, lax.ppermute(own, "particle", middle),
                lax.ppermute(own, "particle", inward), lax.ppermute(own, "particle", beyond)]

        def find(need):
            at = need // 2
            which = jnp.where(at == z, 0, jnp.where(at == 3 - z, 1, jnp.where(at == plane, 2, 3)))
            row = need % 2
            return pick(which, [jnp.where(row == 0, h[0], h[1]) for h in held])

        out = jnp.stack([find(jnp.where(z < 2, chosen[i], chosen[6 + i])) for i in range(2)])
        sent = lax.ppermute(out, "particle", outward)
        inner = (z == 1) | (z == 2)

        def final(slot):
            need = chosen[slot]
            edge = jnp.where(need // 2 == z, jnp.where(need % 2 == 0, own[0], own[1]),
                             jnp.where(slot % 2 == 0, sent[0], sent[1]))
            return jnp.where(inner, find(need), edge)

        mine = final(me)
        got.append((mine, lax.ppermute(final(me ^ 1), "particle", swap)))
    return got


def body(latents, text_kv, ancestors, order, embed_weight, embed_bias, shift, scale,
         qkv_weight, norm_gains, *, particles):
    width = norm_gains.shape[1]
    me = lax.axis_index("particle")
    seq = lax.axis_index("seq")
    chosen = ancestors[order]
    lat = pack(latents[0].astype(BF16))
    kv = text_kv[0]
    if particles == 8:
        x_other, x_mine = route_latents(lat, chosen, me)
        (ka, kb), (va, vb) = route_text(kv, chosen, me, x_mine)
    else:
        need = chosen[me]
        x_mine = lax.all_gather(lat, "particle", axis=0)[need]
        x_other = lax.ppermute(x_mine, "seq", [(0, 1), (1, 0)])
        text = lax.all_gather(kv, "particle", axis=0)[need]
        rows = text.shape[1] // 2
        ka, kb, va, vb = text[0, :rows], text[0, rows:], text[1, :rows], text[1, rows:]
    q, k, v = project(x_other, x_mine, embed_weight, embed_bias, shift, scale, norm_gains, qkv_weight)
    acc0, sum0 = image_attention(q, k, v, 0, width)
    acc1, sum1 = image_attention(q, k, v, 1, width)
    away = text_attention(q, ka, kb, va, vb, acc0, sum0, 0, width)
    theirs = lax.ppermute(away, "seq", [(0, 1), (1, 0)])
    mine = text_attention(q, ka, kb, va, vb, acc1, sum1, 1, width)
    left = jnp.where(seq == 0, mine, theirs)
    right = jnp.where(seq == 0, theirs, mine)
    return jnp.concatenate([left, right], axis=1)[None]


def solution(mesh):
    in_specs = (
        P(("groups", "particle"), "seq", None),
        P(("groups", "particle"), None, None, "seq"),
        P("groups"),
        P("groups"),
        P(),
        P(),
        P("groups"),
        P("groups"),
        P(None, "seq"),
        P(),
    )
    out_specs = P(("groups", "particle"), "seq", None)
    run = functools.partial(body, particles=mesh.shape["particle"])
    return jax.shard_map(run, mesh=mesh, in_specs=in_specs, out_specs=out_specs, check_vma=False)
```

time: 245 us -> 118 us (0.48)
  waiting for transfers between devices: 80.4 us -> 25.1 us
  matrix products: 49.8 us -> 0 us
  Pallas kernels: 0 us -> 44.7 us
  local copies, waits for them, and re-layouts: 42.4 us -> 5.27 us
  blocking collectives: 33.6 us -> 0 us
  starting transfers between devices: 0.22 us -> 30.2 us
  other arithmetic: 22.2 us -> 4.45 us
  between operations: 15.4 us -> 8.01 us
    all_gather x2 -> x0, waiting for transfers between devices: 79.8 us -> none  [the longest x1 75.7 us: body(): lax.all_gather(text_kv, 'particle', axis=0, tiled=True)]
    pallas_call x0 -> x5, Pallas kernels: none -> 44.7 us  [the longest x1 25.6 us: project(): pl.pallas_call(functools.partial(project_kernel, chunk=min(128, x0.shape[...]
    dot_general x3 -> x0, matrix products: 38.6 us -> none  [the longest x1 19.8 us: project_rows(): jnp.einsum('prd,dc->prc', normed, qkv_weight, preferred_element_type=jnp....]
    ppermute x0 -> x19, starting transfers between devices: none -> 30.2 us  [the longest x2 6.45 us: route_text(): lax.ppermute(own, 'particle', inward)]
    all_gather x1 -> x0, blocking collectives: 26.9 us -> none  [body(): lax.all_gather(lat_half, 'particle', axis=0, tiled=True)]
    ppermute x0 -> x19, waiting for transfers between devices: none -> 25.1 us  [the longest x2 8.43 us: route_text(): lax.ppermute(own, 'particle', beyond)]
    unnamed x22 -> x23, local copies, waits for them, and re-layouts: 25.3 us -> 3.96 us
    unnamed x1 -> x0, other arithmetic: 11.4 us -> none
  transfers between devices with their start and end apart: 2 -> 19, of which waited for: 2 -> 7; matrix products, arithmetic and copies ran while one was open for 18% -> 3% of each run, Pallas kernels for 0% -> 35%
where the time goes in v1:
time: 118 us
  Pallas kernels  44.7 us (38%)
  starting transfers between devices  30.2 us (26%)
  waiting for transfers between devices  25.1 us (21%)
  between operations  8.01 us (7%)
  local copies, waits for them, and re-layouts  5.27 us (4%)
  other arithmetic  4.45 us (4%)
    pallas_call x1, Pallas kernels, project(): pl.pallas_call(functools.partial(project_kernel, chunk=min(128, x0.shape[...  25.6 us
    pallas_call x2, Pallas kernels, image_attention(): pl.pallas_call(functools.partial(image_kernel, chunk=256, unit=unit), gri...  11.7 us
    ppermute x2, waiting for transfers between devices, route_text(): lax.ppermute(own, 'particle', beyond)  8.43 us
    pallas_call x2, Pallas kernels, text_attention(): pl.pallas_call(functools.partial(text_kernel, unit=unit), grid=(heads,),...  7.34 us
    ppermute x2, starting transfers between devices, route_text(): lax.ppermute(own, 'particle', inward)  6.45 us
    ppermute x2, waiting for transfers between devices, route_text(): recv = lax.ppermute(give, 'particle', swap)  6.24 us
    ppermute x3, starting transfers between devices, route_latents(): lax.ppermute(lat, 'particle', [(2 * a + b, 2 * ((a + k) % 4) + b) for a i...  5.56 us
    ppermute x2, waiting for transfers between devices, route_text(): got.append((mine, lax.ppermute(final(me ^ 1), 'particle', swap)))  5.35 us
  transfers between devices with their start and end apart: 19, of which 7 were waited for; matrix products, arithmetic and copies ran while one was open for 3% of the time, Pallas kernels for 35%

profile of v1, /device:TPU:1, one launch (start us, length us, event | category | flops | bytes accessed | tf_op | source)
XLA Modules:
  0.0 117.7 jit_solution(10949187590108811295)
XLA Ops:
  0.0 1.1 copy.12
  1.2 2.2 %collective-permute-start.2 = (bf16[256,128]{1,0:T(8,128)(2,1)S(1)}, bf16[256,128]{1,0:T(8,128)(2,1)S(1)}, u32[]{:S(2)}, u32[]{:S(2)}) collective-permute-start(bf16[256,128]{1,0:T(8,128)(2,1)S(1)} %pad_maximum_fusion.4), channel_id=1, source_target_pairs={{0,4},{2,6},{4,8},{6,10},{8,12},{10,14},{12,0},{14,2},{1,5},{3,7},... | collective-permute-start | bytes 196616 | tf_op jit(solution)/shard_map/ppermute | solution.py:165
  3.4 2.3 %collective-permute-start.1 = (bf16[256,128]{1,0:T(8,128)(2,1)S(1)}, bf16[256,128]{1,0:T(8,128)(2,1)S(1)}, u32[]{:S(2)}, u32[]{:S(2)}) collective-permute-start(bf16[256,128]{1,0:T(8,128)(2,1)S(1)} %pad_maximum_fusion.4), channel_id=1, source_target_pairs={{0,8},{2,10},{4,12},{6,14},{8,0},{10,2},{12,4},{14,6},{1,9},{3,11}... | collective-permute-start | bytes 196616 | tf_op jit(solution)/shard_map/ppermute | solution.py:165
  5.7 1.1 collective-permute-start
  11.4 1.3 %collective-permute-start.5 = (bf16[256,128]{1,0:T(8,128)(2,1)S(1)}, bf16[256,128]{1,0:T(8,128)(2,1)S(1)}, u32[]{:S(2)}, u32[]{:S(2)}) collective-permute-start(bf16[256,128]{1,0:T(8,128)(2,1)S(1)} %select_select_fusion.4), channel_id=1, source_target_pairs={{0,2},{2,0},{4,6},{6,4},{8,10},{10,8},{12,14},{14,12},{1,3},{3,1},... | collective-permute-start | bytes 196616 | tf_op jit(solution)/shard_map/ppermute | solution.py:174
  15.1 2.0 %collective-permute-start.4 = (bf16[256,128]{1,0:T(8,128)(2,1)S(1)}, bf16[256,128]{1,0:T(8,128)(2,1)S(1)}, u32[]{:S(2)}, u32[]{:S(2)}) collective-permute-start(bf16[256,128]{1,0:T(8,128)(2,1)S(1)} %select_select_fusion.4), channel_id=1, source_target_pairs={{0,3},{1,2},{2,1},{3,0},{4,7},{5,6},{6,5},{7,4},{8,11},{9,10},{10,... | collective-permute-start | bytes 196616 | tf_op jit(solution)/shard_map/ppermute | solution.py:176
  17.4 1.3 %collective-permute-start.7 = (bf16[128,768]{1,0:T(8,128)(2,1)S(1)}, bf16[128,768]{1,0:T(8,128)(2,1)S(1)}, u32[]{:S(2)}, u32[]{:S(2)}) collective-permute-start(bf16[128,768]{1,0:T(8,128)(2,1)S(1)} %get-tuple-element.33), channel_id=1, source_target_pairs={{0,2},{2,0},{4,6},{6,4},{8,10},{10,8},{12,14},{14,12},{1,3},{3,1},... | collective-permute-start | bytes 589832 | tf_op jit(solution)/shard_map/ppermute | solution.py:196
  21.7 2.0 %collective-permute-done.7 = bf16[128,768]{1,0:T(8,128)(2,1)S(1)} collective-permute-done((bf16[128,768]{1,0:T(8,128)(2,1)S(1)}, bf16[128,768]{1,0:T(8,128)(2,1)S(1)}, u32[]{:S(2)}, u32[]{:S(2)}) %collective-permute-start.7) | collective-permute-done | bytes 196640 | tf_op jit(solution)/shard_map/ppermute | solution.py:196
  23.7 4.2 %collective-permute-done.6 = bf16[128,768]{1,0:T(8,128)(2,1)S(1)} collective-permute-done((bf16[128,768]{1,0:T(8,128)(2,1)S(1)}, bf16[128,768]{1,0:T(8,128)(2,1)S(1)}, u32[]{:S(2)}, u32[]{:S(2)}) %collective-permute-start.6) | collective-permute-done | bytes 196640 | tf_op jit(solution)/shard_map/ppermute | solution.py:196
  28.7 3.7 %collective-permute-start.9 = (bf16[2,128,768]{2,1,0:T(8,128)(2,1)S(1)}, bf16[2,128,768]{2,1,0:T(8,128)(2,1)S(1)}, u32[]{:S(2)}, u32[]{:S(2)}) collective-permute-start(bf16[2,128,768]{2,1,0:T(8,128)(2,1)S(1)} %get-tuple-element.15), channel_id=1, source_target_pairs={{0,4},{2,6},{12,8},{14,10},{1,5},{3,7},{13,9},{15,11},{16,20},{18,... | collective-permute-start | bytes 1179656 | tf_op jit(solution)/shard_map/ppermute | solution.py:202
  32.4 2.4 %collective-permute-start.8 = (bf16[2,128,768]{2,1,0:T(8,128)(2,1)S(1)}, bf16[2,128,768]{2,1,0:T(8,128)(2,1)S(1)}, u32[]{:S(2)}, u32[]{:S(2)}) collective-permute-start(bf16[2,128,768]{2,1,0:T(8,128)(2,1)S(1)} %get-tuple-element.15), channel_id=1, source_target_pairs={{0,8},{2,10},{12,4},{14,6},{1,9},{3,11},{13,5},{15,7},{16,24},{18,... | collective-permute-start | bytes 1179656 | tf_op jit(solution)/shard_map/ppermute | solution.py:202
  34.8 25.6 %project.1 = (bf16[1024,768]{1,0:T(8,128)(2,1)S(1)}, bf16[1024,768]{1,0:T(8,128)(2,1)S(1)}, bf16[1024,768]{1,0:T(8,128)(2,1)S(1)}) custom-call(bf16[256,128]{1,0:T(8,128)(2,1)S(1)} %broadcast_select_fusion.5.x0_ref, bf16[256,128]{1,0:T(8,128)(2,1)S(1)} %get-tuple-element.23.x1_ref, bf16[64,3072]{1,0:T(8,128)(2,1)S(1)} %copy-done.1, f32[1,3072]{1,0:T(1,128)S(1)} %bitcast.49, ...), custom_call_target="tpu_custom_call" | custom-call | flops 14495514624 | bytes 18874368 | tf_op jit(solution)/shard_map/project/pallas_call | solution.py:65
  61.2 2.8 %collective-permute-start.14 = (bf16[2,128,768]{2,1,0:T(8,128)(2,1)S(1)}, bf16[2,128,768]{2,1,0:T(8,128)(2,1)S(1)}, u32[]{:S(2)}, u32[]{:S(2)}) collective-permute-start(bf16[2,128,768]{2,1,0:T(8,128)(2,1)S(1)} %get-tuple-element.16), channel_id=1, source_target_pairs={{0,4},{2,6},{12,8},{14,10},{1,5},{3,7},{13,9},{15,11},{16,20},{18,... | collective-permute-start | bytes 1179656 | tf_op jit(solution)/shard_map/ppermute | solution.py:202
  64.0 1.3 %collective-permute-start.13 = (bf16[2,128,768]{2,1,0:T(8,128)(2,1)S(1)}, bf16[2,128,768]{2,1,0:T(8,128)(2,1)S(1)}, u32[]{:S(2)}, u32[]{:S(2)}) collective-permute-start(bf16[2,128,768]{2,1,0:T(8,128)(2,1)S(1)} %get-tuple-element.16), channel_id=1, source_target_pairs={{0,8},{2,10},{12,4},{14,6},{1,9},{3,11},{13,5},{15,7},{16,24},{18,... | collective-permute-start | bytes 1179656 | tf_op jit(solution)/shard_map/ppermute | solution.py:202
  65.6 1.3 %collective-permute-start.11 = (bf16[2,128,768]{2,1,0:T(8,128)(2,1)S(1)}, bf16[2,128,768]{2,1,0:T(8,128)(2,1)S(1)}, u32[]{:S(2)}, u32[]{:S(2)}) collective-permute-start(bf16[2,128,768]{2,1,0:T(8,128)(2,1)S(1)} %pad_maximum_fusion.2), channel_id=1, source_target_pairs={{4,0},{6,2},{8,12},{10,14},{5,1},{7,3},{9,13},{11,15},{20,16},{22,... | collective-permute-start | bytes 1179656 | tf_op jit(solution)/shard_map/ppermute | solution.py:211
  66.9 3.8 %collective-permute-done.14 = bf16[2,128,768]{2,1,0:T(8,128)(2,1)S(1)} collective-permute-done((bf16[2,128,768]{2,1,0:T(8,128)(2,1)S(1)}, bf16[2,128,768]{2,1,0:T(8,128)(2,1)S(1)}, u32[]{:S(2)}, u32[]{:S(2)}) %collective-permute-start.14) | collective-permute-done | bytes 393248 | tf_op jit(solution)/shard_map/ppermute | solution.py:202
  70.6 8.4 %collective-permute-done.13 = bf16[2,128,768]{2,1,0:T(8,128)(2,1)S(1)} collective-permute-done((bf16[2,128,768]{2,1,0:T(8,128)(2,1)S(1)}, bf16[2,128,768]{2,1,0:T(8,128)(2,1)S(1)}, u32[]{:S(2)}, u32[]{:S(2)}) %collective-permute-start.13) | collective-permute-done | bytes 393248 | tf_op jit(solution)/shard_map/ppermute | solution.py:202
  79.3 1.5 %collective-permute-start.16 = (bf16[2,128,768]{2,1,0:T(8,128)(2,1)S(1)}, bf16[2,128,768]{2,1,0:T(8,128)(2,1)S(1)}, u32[]{:S(2)}, u32[]{:S(2)}) collective-permute-start(bf16[2,128,768]{2,1,0:T(8,128)(2,1)S(1)} %pad_maximum_fusion.3), channel_id=1, source_target_pairs={{4,0},{6,2},{8,12},{10,14},{5,1},{7,3},{9,13},{11,15},{20,16},{22,... | collective-permute-start | bytes 1179656 | tf_op jit(solution)/shard_map/ppermute | solution.py:211
  80.8 5.9 %image_0.1 = (f32[512,768]{1,0:T(8,128)S(1)}, f32[512,768]{1,0:T(8,128)S(1)}) custom-call(bf16[1024,768]{1,0:T(8,128)(2,1)S(1)} %get-tuple-element.14.q_ref, bf16[1024,768]{1,0:T(8,128)(2,1)S(1)} %get-tuple-element.17.k_ref, bf16[1024,768]{1,0:T(8,128)(2,1)S(1)} %get-tuple-element.18.v_ref), custom_call_target="tpu_custom_call" | custom-call | flops 3221225472 | bytes 7864320 | tf_op jit(solution)/shard_map/image_0/pallas_call | solution.py:99
  86.9 1.3 %collective-permute-start.12 = (bf16[128,768]{1,0:T(8,128)(2,1)S(1)}, bf16[128,768]{1,0:T(8,128)(2,1)S(1)}, u32[]{:S(2)}, u32[]{:S(2)}) collective-permute-start(bf16[128,768]{1,0:T(8,128)(2,1)S(1)} %select_bitcast_fusion.2), channel_id=1, source_target_pairs={{0,2},{2,0},{4,6},{6,4},{8,10},{10,8},{12,14},{14,12},{1,3},{3,1},... | collective-permute-start | bytes 589832 | tf_op jit(solution)/shard_map/ppermute | solution.py:221
  88.2 1.3 %collective-permute-done.16 = bf16[2,128,768]{2,1,0:T(8,128)(2,1)S(1)} collective-permute-done((bf16[2,128,768]{2,1,0:T(8,128)(2,1)S(1)}, bf16[2,128,768]{2,1,0:T(8,128)(2,1)S(1)}, u32[]{:S(2)}, u32[]{:S(2)}) %collective-permute-start.16) | collective-permute-done | bytes 393248 | tf_op jit(solution)/shard_map/ppermute | solution.py:211
  89.6 1.1 collective-permute-start.17
  90.9 0.9 collective-permute-done.12.kb_ref
  91.7 4.5 %collective-permute-done.17.vb_ref = bf16[128,768]{1,0:T(8,128)(2,1)S(1)} collective-permute-done((bf16[128,768]{1,0:T(8,128)(2,1)S(1)}, bf16[128,768]{1,0:T(8,128)(2,1)S(1)}, u32[]{:S(2)}, u32[]{:S(2)}) %collective-permute-start.17) | collective-permute-done | bytes 196640 | tf_op jit(solution)/shard_map/ppermute | solution.py:221
  96.2 3.7 %text_0.1 = bf16[512,768]{1,0:T(8,128)(2,1)S(1)} custom-call(bf16[1024,768]{1,0:T(8,128)(2,1)S(1)} %get-tuple-element.14.q_ref, bf16[128,768]{1,0:T(8,128)(2,1)S(1)} %select_bitcast_fusion.3.ka_ref, bf16[128,768]{1,0:T(8,128)(2,1)S(1)} %collective-permute-done.12.kb_ref, bf16[128,768]{1,0:T(8,128)(2,1)S(1)} %select_bitcast_fusion.1.va_ref, ...), custom_call_target="tpu_custom_call" | custom-call | flops 805306368 | bytes 5505024 | tf_op jit(solution)/shard_map/text_0/pallas_call | solution.py:135
  99.9 2.9 %collective-permute-start.18 = (bf16[512,768]{1,0:T(8,128)(2,1)S(1)}, bf16[512,768]{1,0:T(8,128)(2,1)}, u32[]{:S(2)}, u32[]{:S(2)}) collective-permute-start(bf16[512,768]{1,0:T(8,128)(2,1)S(1)} %text_0.1), channel_id=1, source_target_pairs={{0,1},{1,0},{2,3},{3,2},{4,5},{5,4},{6,7},{7,6},{8,9},{9,8},{10,11... | collective-permute-start | bytes 2359304 | tf_op jit(solution)/shard_map/ppermute | solution.py:247
  102.8 1.4 %copy-done.7 = bf16[1024,768]{1,0:T(8,128)(2,1)S(1)} copy-done((bf16[1024,768]{1,0:T(8,128)(2,1)S(1)}, bf16[1024,768]{1,0:T(8,128)(2,1)}, u32[]{:S(2)}) %copy-start.7) | copy-done | bytes 1572888
  104.2 1.4 %copy-done.9 = bf16[1024,768]{1,0:T(8,128)(2,1)S(1)} copy-done((bf16[1024,768]{1,0:T(8,128)(2,1)S(1)}, bf16[1024,768]{1,0:T(8,128)(2,1)}, u32[]{:S(2)}) %copy-start.9) | copy-done | bytes 1572888
  105.6 5.8 %image_1.1 = (f32[512,768]{1,0:T(8,128)S(1)}, f32[512,768]{1,0:T(8,128)S(1)}) custom-call(bf16[1024,768]{1,0:T(8,128)(2,1)S(1)} %get-tuple-element.14.q_ref, bf16[1024,768]{1,0:T(8,128)(2,1)S(1)} %copy-done.7, bf16[1024,768]{1,0:T(8,128)(2,1)S(1)} %copy-done.9), custom_call_target="tpu_custom_call" | custom-call | flops 3221225472 | bytes 7864320 | tf_op jit(solution)/shard_map/image_1/pallas_call | solution.py:99
  111.5 3.7 %text_1.1 = bf16[512,768]{1,0:T(8,128)(2,1)S(1)} custom-call(bf16[1024,768]{1,0:T(8,128)(2,1)S(1)} %get-tuple-element.14.q_ref, bf16[128,768]{1,0:T(8,128)(2,1)S(1)} %select_bitcast_fusion.3.ka_ref, bf16[128,768]{1,0:T(8,128)(2,1)S(1)} %collective-permute-done.12.kb_ref, bf16[128,768]{1,0:T(8,128)(2,1)S(1)} %select_bitcast_fusion.1.va_ref, ...), custom_call_target="tpu_custom_call" | custom-call | flops 805306368 | bytes 5505024 | tf_op jit(solution)/shard_map/text_1/pallas_call | solution.py:135
  115.2 1.2 %broadcast_select_fusion.1 = (bf16[512,768]{1,0:T(8,128)(2,1)S(1)}, bf16[512,768]{1,0:T(8,128)(2,1)S(1)}) fusion(bf16[512,768]{1,0:T(8,128)(2,1)S(1)} %text_1.1, bf16[512,768]{1,0:T(8,128)(2,1)} %collective-permute-done.18, pred[]{:T(512)S(6)} %eq.102), kind=kLoop, calls=%fused_computation.3 | loop fusion | flops 786432 | bytes 3145729 | tf_op jit(solution)/shard_map/jit(_where)/select_n | solution.py:249
  116.4 1.3 %maximum_bitcast_fusion = bf16[1,512,1536]{2,1,0:T(8,128)(2,1)} fusion(bf16[512,768]{1,0:T(8,128)(2,1)S(1)} %get-tuple-element.26, bf16[512,768]{1,0:T(8,128)(2,1)S(1)} %get-tuple-element.25), kind=kLoop, calls=%fused_computation.1 | loop fusion | flops 3145728 | bytes 3145728 | tf_op jit(solution)/shard_map/broadcast_in_dim | solution.py:251
  (58 shorter events, 5.2 us)
Async XLA Ops:
  0.0 7.5 %copy-start = (s32[8]{0:T(128)S(1)}, s32[8]{0:T(128)}, u32[]{:S(2)}) copy-start(s32[8]{0:T(128)} %param.12) | copy-start | bytes 100
  0.0 17.3 %copy-start.10 = (bf16[1,2,256,768]{3,2,1,0:T(8,128)(2,1)S(1)}, bf16[1,2,256,768]{3,2,1,0:T(8,128)(2,1)}, u32[]{:S(2)}) copy-start(bf16[1,2,256,768]{3,2,1,0:T(8,128)(2,1)} %param.11) | copy-start | bytes 2359300
  1.2 10.1 %collective-permute-start.2 = (bf16[256,128]{1,0:T(8,128)(2,1)S(1)}, bf16[256,128]{1,0:T(8,128)(2,1)S(1)}, u32[]{:S(2)}, u32[]{:S(2)}) collective-permute-start(bf16[256,128]{1,0:T(8,128)(2,1)S(1)} %pad_maximum_fusion.4), channel_id=1, source_target_pairs={{0,4},{2,6},{4,8},{6,10},{8,12},{10,14},{12,0},{14,2},{1,5},{3,7},... | collective-permute-start | bytes 196616 | tf_op jit(solution)/shard_map/ppermute | solution.py:165
  3.4 8.0 %collective-permute-start.1 = (bf16[256,128]{1,0:T(8,128)(2,1)S(1)}, bf16[256,128]{1,0:T(8,128)(2,1)S(1)}, u32[]{:S(2)}, u32[]{:S(2)}) collective-permute-start(bf16[256,128]{1,0:T(8,128)(2,1)S(1)} %pad_maximum_fusion.4), channel_id=1, source_target_pairs={{0,8},{2,10},{4,12},{6,14},{8,0},{10,2},{12,4},{14,6},{1,9},{3,11}... | collective-permute-start | bytes 196616 | tf_op jit(solution)/shard_map/ppermute | solution.py:165
  5.7 5.7 %collective-permute-start = (bf16[256,128]{1,0:T(8,128)(2,1)S(1)}, bf16[256,128]{1,0:T(8,128)(2,1)S(1)}, u32[]{:S(2)}, u32[]{:S(2)}) collective-permute-start(bf16[256,128]{1,0:T(8,128)(2,1)S(1)} %pad_maximum_fusion.4), channel_id=1, source_target_pairs={{0,12},{2,14},{4,0},{6,2},{8,4},{10,6},{12,8},{14,10},{1,13},{3,15... | collective-permute-start | bytes 196616 | tf_op jit(solution)/shard_map/ppermute | solution.py:165
  11.4 5.6 %collective-permute-start.5 = (bf16[256,128]{1,0:T(8,128)(2,1)S(1)}, bf16[256,128]{1,0:T(8,128)(2,1)S(1)}, u32[]{:S(2)}, u32[]{:S(2)}) collective-permute-start(bf16[256,128]{1,0:T(8,128)(2,1)S(1)} %select_select_fusion.4), channel_id=1, source_target_pairs={{0,2},{2,0},{4,6},{6,4},{8,10},{10,8},{12,14},{14,12},{1,3},{3,1},... | collective-permute-start | bytes 196616 | tf_op jit(solution)/shard_map/ppermute | solution.py:174
  15.1 6.5 %collective-permute-start.4 = (bf16[256,128]{1,0:T(8,128)(2,1)S(1)}, bf16[256,128]{1,0:T(8,128)(2,1)S(1)}, u32[]{:S(2)}, u32[]{:S(2)}) collective-permute-start(bf16[256,128]{1,0:T(8,128)(2,1)S(1)} %select_select_fusion.4), channel_id=1, source_target_pairs={{0,3},{1,2},{2,1},{3,0},{4,7},{5,6},{6,5},{7,4},{8,11},{9,10},{10,... | collective-permute-start | bytes 196616 | tf_op jit(solution)/shard_map/ppermute | solution.py:176
  17.1 4.5 %collective-permute-start.3 = (bf16[256,128]{1,0:T(8,128)(2,1)S(1)}, bf16[256,128]{1,0:T(8,128)(2,1)S(1)}, u32[]{:S(2)}, u32[]{:S(2)}) collective-permute-start(bf16[256,128]{1,0:T(8,128)(2,1)S(1)} %get-tuple-element.24), channel_id=1, source_target_pairs={{0,1},{1,0},{2,3},{3,2},{4,5},{5,4},{6,7},{7,6},{8,9},{9,8},{10,11... | collective-permute-start | bytes 196616 | tf_op jit(solution)/shard_map/ppermute | solution.py:175
  17.4 6.3 %collective-permute-start.7 = (bf16[128,768]{1,0:T(8,128)(2,1)S(1)}, bf16[128,768]{1,0:T(8,128)(2,1)S(1)}, u32[]{:S(2)}, u32[]{:S(2)}) collective-permute-start(bf16[128,768]{1,0:T(8,128)(2,1)S(1)} %get-tuple-element.33), channel_id=1, source_target_pairs={{0,2},{2,0},{4,6},{6,4},{8,10},{10,8},{12,14},{14,12},{1,3},{3,1},... | collective-permute-start | bytes 589832 | tf_op jit(solution)/shard_map/ppermute | solution.py:196
  18.7 9.2 %collective-permute-start.6 = (bf16[128,768]{1,0:T(8,128)(2,1)S(1)}, bf16[128,768]{1,0:T(8,128)(2,1)S(1)}, u32[]{:S(2)}, u32[]{:S(2)}) collective-permute-start(bf16[128,768]{1,0:T(8,128)(2,1)S(1)} %get-tuple-element.34), channel_id=1, source_target_pairs={{0,2},{2,0},{4,6},{6,4},{8,10},{10,8},{12,14},{14,12},{1,3},{3,1},... | collective-permute-start | bytes 589832 | tf_op jit(solution)/shard_map/ppermute | solution.py:196
  21.6 13.2 %copy-start.1 = (bf16[64,3072]{1,0:T(8,128)(2,1)S(1)}, bf16[64,3072]{1,0:T(8,128)(2,1)}, u32[]{:S(2)}) copy-start(bf16[64,3072]{1,0:T(8,128)(2,1)} %ew_ref.1) | copy-start | bytes 1179652
  21.6 13.2 %copy-start.2 = (f32[3072]{0:T(1024)S(1)}, f32[3072]{0:T(1024)}, u32[]{:S(2)}) copy-start(f32[3072]{0:T(1024)} %param.15) | copy-start | bytes 36868
  21.6 13.2 %copy-start.3 = (f32[3072]{0:T(1024)S(1)}, f32[3072]{0:T(1024)}, u32[]{:S(2)}) copy-start(f32[3072]{0:T(1024)} %param.16) | copy-start | bytes 36868
  21.6 13.2 %copy-start.4 = (f32[3072]{0:T(1024)S(1)}, f32[3072]{0:T(1024)}, u32[]{:S(2)}) copy-start(f32[3072]{0:T(1024)} %param.17) | copy-start | bytes 36868
  21.7 13.2 %copy-start.5 = (f32[2,128]{1,0:T(2,128)S(1)}, f32[2,128]{1,0:T(2,128)}, u32[]{:S(2)}) copy-start(f32[2,128]{1,0:T(2,128)} %gain_ref.1) | copy-start | bytes 3076
  28.1 35.9 %collective-permute-start.10 = (bf16[2,128,768]{2,1,0:T(8,128)(2,1)S(1)}, bf16[2,128,768]{2,1,0:T(8,128)(2,1)S(1)}, u32[]{:S(2)}, u32[]{:S(2)}) collective-permute-start(bf16[2,128,768]{2,1,0:T(8,128)(2,1)S(1)} %get-tuple-element.15), channel_id=1, source_target_pairs={{4,8},{6,10},{8,4},{10,6},{5,9},{7,11},{9,5},{11,7},{20,24},{22,26... | collective-permute-start | bytes 1179656 | tf_op jit(solution)/shard_map/ppermute | solution.py:201
  28.7 36.6 %collective-permute-start.9 = (bf16[2,128,768]{2,1,0:T(8,128)(2,1)S(1)}, bf16[2,128,768]{2,1,0:T(8,128)(2,1)S(1)}, u32[]{:S(2)}, u32[]{:S(2)}) collective-permute-start(bf16[2,128,768]{2,1,0:T(8,128)(2,1)S(1)} %get-tuple-element.15), channel_id=1, source_target_pairs={{0,4},{2,6},{12,8},{14,10},{1,5},{3,7},{13,9},{15,11},{16,20},{18,... | collective-permute-start | bytes 1179656 | tf_op jit(solution)/shard_map/ppermute | solution.py:202
  32.4 32.9 %collective-permute-start.8 = (bf16[2,128,768]{2,1,0:T(8,128)(2,1)S(1)}, bf16[2,128,768]{2,1,0:T(8,128)(2,1)S(1)}, u32[]{:S(2)}, u32[]{:S(2)}) collective-permute-start(bf16[2,128,768]{2,1,0:T(8,128)(2,1)S(1)} %get-tuple-element.15), channel_id=1, source_target_pairs={{0,8},{2,10},{12,4},{14,6},{1,9},{3,11},{13,5},{15,7},{16,24},{18,... | collective-permute-start | bytes 1179656 | tf_op jit(solution)/shard_map/ppermute | solution.py:202
  60.5 20.4 %copy-start.6 = (bf16[1024,768]{1,0:T(8,128)(2,1)}, bf16[1024,768]{1,0:T(8,128)(2,1)S(1)}, u32[]{:S(2)}) copy-start(bf16[1024,768]{1,0:T(8,128)(2,1)S(1)} %get-tuple-element.17.k_ref) | copy-start | bytes 4718596
  60.5 20.4 %copy-start.8 = (bf16[1024,768]{1,0:T(8,128)(2,1)}, bf16[1024,768]{1,0:T(8,128)(2,1)S(1)}, u32[]{:S(2)}) copy-start(bf16[1024,768]{1,0:T(8,128)(2,1)S(1)} %get-tuple-element.18.v_ref) | copy-start | bytes 4718596
  60.5 6.4 %collective-permute-start.15 = (bf16[2,128,768]{2,1,0:T(8,128)(2,1)S(1)}, bf16[2,128,768]{2,1,0:T(8,128)(2,1)S(1)}, u32[]{:S(2)}, u32[]{:S(2)}) collective-permute-start(bf16[2,128,768]{2,1,0:T(8,128)(2,1)S(1)} %get-tuple-element.16), channel_id=1, source_target_pairs={{4,8},{6,10},{8,4},{10,6},{5,9},{7,11},{9,5},{11,7},{20,24},{22,26... | collective-permute-start | bytes 1179656 | tf_op jit(solution)/shard_map/ppermute | solution.py:201
  61.2 9.5 %collective-permute-start.14 = (bf16[2,128,768]{2,1,0:T(8,128)(2,1)S(1)}, bf16[2,128,768]{2,1,0:T(8,128)(2,1)S(1)}, u32[]{:S(2)}, u32[]{:S(2)}) collective-permute-start(bf16[2,128,768]{2,1,0:T(8,128)(2,1)S(1)} %get-tuple-element.16), channel_id=1, source_target_pairs={{0,4},{2,6},{12,8},{14,10},{1,5},{3,7},{13,9},{15,11},{16,20},{18,... | collective-permute-start | bytes 1179656 | tf_op jit(solution)/shard_map/ppermute | solution.py:202
  64.0 15.1 %collective-permute-start.13 = (bf16[2,128,768]{2,1,0:T(8,128)(2,1)S(1)}, bf16[2,128,768]{2,1,0:T(8,128)(2,1)S(1)}, u32[]{:S(2)}, u32[]{:S(2)}) collective-permute-start(bf16[2,128,768]{2,1,0:T(8,128)(2,1)S(1)} %get-tuple-element.16), channel_id=1, source_target_pairs={{0,8},{2,10},{12,4},{14,6},{1,9},{3,11},{13,5},{15,7},{16,24},{18,... | collective-permute-start | bytes 1179656 | tf_op jit(solution)/shard_map/ppermute | solution.py:202
  65.6 21.2 %collective-permute-start.11 = (bf16[2,128,768]{2,1,0:T(8,128)(2,1)S(1)}, bf16[2,128,768]{2,1,0:T(8,128)(2,1)S(1)}, u32[]{:S(2)}, u32[]{:S(2)}) collective-permute-start(bf16[2,128,768]{2,1,0:T(8,128)(2,1)S(1)} %pad_maximum_fusion.2), channel_id=1, source_target_pairs={{4,0},{6,2},{8,12},{10,14},{5,1},{7,3},{9,13},{11,15},{20,16},{22,... | collective-permute-start | bytes 1179656 | tf_op jit(solution)/shard_map/ppermute | solution.py:211
  79.3 10.1 %collective-permute-start.16 = (bf16[2,128,768]{2,1,0:T(8,128)(2,1)S(1)}, bf16[2,128,768]{2,1,0:T(8,128)(2,1)S(1)}, u32[]{:S(2)}, u32[]{:S(2)}) collective-permute-start(bf16[2,128,768]{2,1,0:T(8,128)(2,1)S(1)} %pad_maximum_fusion.3), channel_id=1, source_target_pairs={{4,0},{6,2},{8,12},{10,14},{5,1},{7,3},{9,13},{11,15},{20,16},{22,... | collective-permute-start | bytes 1179656 | tf_op jit(solution)/shard_map/ppermute | solution.py:211
  86.9 4.9 %collective-permute-start.12 = (bf16[128,768]{1,0:T(8,128)(2,1)S(1)}, bf16[128,768]{1,0:T(8,128)(2,1)S(1)}, u32[]{:S(2)}, u32[]{:S(2)}) collective-permute-start(bf16[128,768]{1,0:T(8,128)(2,1)S(1)} %select_bitcast_fusion.2), channel_id=1, source_target_pairs={{0,2},{2,0},{4,6},{6,4},{8,10},{10,8},{12,14},{14,12},{1,3},{3,1},... | collective-permute-start | bytes 589832 | tf_op jit(solution)/shard_map/ppermute | solution.py:221
  89.6 6.7 %collective-permute-start.17 = (bf16[128,768]{1,0:T(8,128)(2,1)S(1)}, bf16[128,768]{1,0:T(8,128)(2,1)S(1)}, u32[]{:S(2)}, u32[]{:S(2)}) collective-permute-start(bf16[128,768]{1,0:T(8,128)(2,1)S(1)} %select_bitcast_fusion), channel_id=1, source_target_pairs={{0,2},{2,0},{4,6},{6,4},{8,10},{10,8},{12,14},{14,12},{1,3},{3,1},... | collective-permute-start | bytes 589832 | tf_op jit(solution)/shard_map/ppermute | solution.py:221
  99.9 15.2 %collective-permute-start.18 = (bf16[512,768]{1,0:T(8,128)(2,1)S(1)}, bf16[512,768]{1,0:T(8,128)(2,1)}, u32[]{:S(2)}, u32[]{:S(2)}) collective-permute-start(bf16[512,768]{1,0:T(8,128)(2,1)S(1)} %text_0.1), channel_id=1, source_target_pairs={{0,1},{1,0},{2,3},{3,2},{4,5},{5,4},{6,7},{7,6},{8,9},{9,8},{10,11... | collective-permute-start | bytes 2359304 | tf_op jit(solution)/shard_map/ppermute | solution.py:247
  102.8 1.4 %copy-start.7 = (bf16[1024,768]{1,0:T(8,128)(2,1)S(1)}, bf16[1024,768]{1,0:T(8,128)(2,1)}, u32[]{:S(2)}) copy-start(bf16[1024,768]{1,0:T(8,128)(2,1)} %copy-done.6) | copy-start | bytes 4718596
  104.2 1.4 %copy-start.9 = (bf16[1024,768]{1,0:T(8,128)(2,1)S(1)}, bf16[1024,768]{1,0:T(8,128)(2,1)}, u32[]{:S(2)}) copy-start(bf16[1024,768]{1,0:T(8,128)(2,1)} %copy-done.8) | copy-start | bytes 4718596

commit v2 on v1

--- a/solution.py
+++ b/solution.py
@@ -78,7 +78,7 @@
     )(*small, weight)
 
 
-def image_kernel(q_ref, k_ref, v_ref, acc_ref, sum_ref, *, chunk, unit):
+def image_alone_kernel(q_ref, k_ref, v_ref, acc_ref, sum_ref, *, chunk, unit):
     width = k_ref.shape[1]
     vals = jnp.concatenate([v_ref[...], jnp.ones_like(v_ref)], axis=1)
     for at in range(0, q_ref.shape[0], chunk):
@@ -90,24 +90,18 @@
         sum_ref[r, :] = o[:, width:]
 
 
-def image_attention(q, k, v, half, width):
+def image_alone(q, k, v, width):
     tokens, cols = q.shape
-    rows = tokens // 2
-    heads = cols // width
-    unit = LOG2E / width ** 0.5
-    out = jax.ShapeDtypeStruct((rows, cols), F32)
-    return pl.pallas_call(
-        functools.partial(image_kernel, chunk=256, unit=unit),
-        grid=(heads,),
-        in_specs=[pl.BlockSpec((rows, width), lambda h: (half, h))]
-        + [pl.BlockSpec((tokens, width), lambda h: (0, h))] * 2,
-        out_specs=[pl.BlockSpec((rows, width), lambda h: (0, h))] * 2,
+    head = pl.BlockSpec((tokens, width), lambda h: (0, h))
+    out = jax.ShapeDtypeStruct((tokens, cols), F32)
+    return pl.pallas_call(
+        functools.partial(image_alone_kernel, chunk=256, unit=LOG2E / width ** 0.5),
+        grid=(cols // width,),
+        in_specs=[head] * 3,
+        out_specs=[head] * 2,
         out_shape=[out] * 2,
         compiler_params=pltpu.CompilerParams(vmem_limit_bytes=32 * 1024 * 1024),
-        cost_estimate=pl.CostEstimate(
-            flops=8 * rows * tokens * cols, bytes_accessed=6 * tokens * cols + 8 * rows * cols,
-            transcendentals=rows * tokens * heads),
-        name=f"image_{half}",
+        name="image_alone",
     )(q, k, v)
 
 
@@ -135,7 +129,8 @@
     return pl.pallas_call(
         functools.partial(text_kernel, unit=unit),
         grid=(heads,),
-        in_specs=[pl.BlockSpec((rows, width), lambda h: (half, h))] + [part] * 4 + [full] * 2,
+        in_specs=[pl.BlockSpec((rows, width), lambda h: (half, h))] + [part] * 4
+        + [pl.BlockSpec((rows, width), lambda h: (half, h))] * 2,
         out_specs=full,
         out_shape=jax.ShapeDtypeStruct((rows, cols), BF16),
         compiler_params=pltpu.CompilerParams(vmem_limit_bytes=32 * 1024 * 1024),
@@ -151,101 +146,230 @@
     return jnp.concatenate([lat[:rows], lat[rows:]], axis=1)
 
 
-def pick(which, choices):
-    res = choices[0]
-    for i, item in enumerate(choices[1:], 1):
-        res = jnp.where(which == i, item, res)
-    return res
-
-
-def route_latents(lat, chosen, me):
+MESH = pl.DeviceIdType.MESH
+
+
+def greet(peers):
+    barrier = pltpu.get_barrier_semaphore()
+    for peer in peers:
+        pl.semaphore_signal(barrier, inc=1, device_id=peer, device_id_type=MESH)
+    pl.semaphore_wait(barrier, len(peers))
+
+
+def gather_kernel(anc_ref, ord_ref, lat_ref, kv_ref, other_ref, mine_ref, plane_ref,
+                  held, give, keep, send, recv, local):
+    g, me, s = lax.axis_index("groups"), lax.axis_index("particle"), lax.axis_index("seq")
     z, y = me // 2, me % 2
-    held = [lat]
-    for k in (1, 2, 3):
-        held.append(lax.ppermute(
-            lat, "particle", [(2 * a + b, 2 * ((a + k) % 4) + b) for a in range(4) for b in range(2)]))
-    need = chosen[me]
-    other = chosen[me ^ 1]
-    mine = pick((z - need // 2) % 4, held)
-    theirs = pick((z - other // 2) % 4, held)
-    swap = [(p, p ^ 1) for p in range(8)]
-    flip = [(0, 1), (1, 0)]
-    diag = [(2 * p + s, 2 * (p ^ 1) + (1 - s)) for p in range(8) for s in range(2)]
-    from_y = lax.ppermute(theirs, "particle", swap)
-    from_seq = lax.ppermute(mine, "seq", flip)
-    from_diag = lax.ppermute(theirs, ("particle", "seq"), diag)
-    here = need % 2 == y
-    return jnp.where(here, from_seq, from_diag), jnp.where(here, mine, from_y)
-
-
-def route_text(kv, chosen, me, after):
-    z, y = me // 2, me % 2
-    swap = [(p, p ^ 1) for p in range(8)]
+    across = (g, 2 * z + 1 - y, s)
+    core = (g, me, 1 - s)
+    diag = (g, 2 * z + 1 - y, 1 - s)
+    planes = [(g, 2 * ((z + k) % 4) + y, s) for k in (1, 2, 3)]
+    greet(planes + [across, core, diag])
+
+    def push(src, dst, i, peer):
+        return pltpu.make_async_remote_copy(
+            src_ref=src, dst_ref=dst, send_sem=send.at[i], recv_sem=recv.at[i],
+            device_id=peer, device_id_type=MESH)
+
+    first = [push(lat_ref, held.at[k], k - 1, planes[k - 1]) for k in (1, 2, 3)]
+    for copy in first:
+        copy.start()
+    rows = kv_ref.shape[1] // 2
+    text = push(kv_ref.at[:, pl.ds(pl.multiple_of((1 - y) * rows, rows), rows)],
+                plane_ref.at[:, y], 3, across)
+    text.start()
+    own = pltpu.make_async_copy(
+        kv_ref.at[:, pl.ds(pl.multiple_of(y * rows, rows), rows)], plane_ref.at[:, y], local)
+    own.start()
+    held[0] = lat_ref[...]
+    need = anc_ref[ord_ref[me]]
+    wish = anc_ref[ord_ref[2 * z + 1 - y]]
+    for copy in first:
+        copy.wait()
+    keep[0] = held[(z + 4 - need // 2) % 4]
+    give[...] = held[(z + 4 - wish // 2) % 4]
+    second = [push(give, keep.at[1], 4, across), push(keep.at[0], keep.at[2], 5, core),
+              push(give, keep.at[3], 6, diag)]
+    for copy in second:
+        copy.start()
+    for copy in second:
+        copy.wait()
+    turn = (need % 2 + y) % 2
+    mine_ref[...] = keep[turn]
+    other_ref[...] = keep[2 + turn]
+    text.wait()
+    own.wait()
+
+
+def gather(ancestors, order, lat, kv):
+    block = jax.ShapeDtypeStruct(lat.shape, lat.dtype)
+    two, rows, cols = kv.shape
+    vmem = pl.BlockSpec(memory_space=pltpu.VMEM)
+    smem = pl.BlockSpec(memory_space=pltpu.SMEM)
+    anyp = pl.BlockSpec(memory_space=pl.ANY)
+    return pl.pallas_call(
+        gather_kernel,
+        in_specs=[smem, smem, vmem, anyp],
+        out_specs=[vmem, vmem, anyp],
+        out_shape=[block, block, jax.ShapeDtypeStruct((two, 2, rows // 2, cols), kv.dtype)],
+        scratch_shapes=[pltpu.VMEM((4,) + lat.shape, lat.dtype), pltpu.VMEM(lat.shape, lat.dtype),
+                        pltpu.VMEM((4,) + lat.shape, lat.dtype),
+                        pltpu.SemaphoreType.DMA((7,)), pltpu.SemaphoreType.DMA((7,)),
+                        pltpu.SemaphoreType.DMA],
+        compiler_params=pltpu.CompilerParams(
+            collective_id=0, has_side_effects=True, vmem_limit_bytes=16 * 1024 * 1024),
+        cost_estimate=pl.CostEstimate(flops=0, bytes_accessed=20000000, transcendentals=0),
+        name="gather",
+    )(ancestors, order, lat, kv)
+
+
+def inward_planes(planes):
     middle = [(2, 4), (3, 5), (4, 2), (5, 3)]
     inward = [(0, 2), (1, 3), (6, 4), (7, 5)]
     beyond = [(0, 4), (1, 5), (6, 2), (7, 3)]
-    outward = [(2, 0), (3, 1), (4, 6), (5, 7)]
-    rows = kv.shape[1] // 2
-    got = []
-    plane = jnp.where(z < 2, 0, 3)
-    planes = []
-    for c in range(2):
-        halves = kv[c].reshape(2, rows, kv.shape[2])
-        own = jnp.where(y == 0, halves[0], halves[1])
-        give = jnp.where(y == 0, halves[1], halves[0])
-        recv = lax.ppermute(give, "particle", swap)
-        planes.append(jnp.stack([jnp.where(y == 0, own, recv), jnp.where(y == 0, recv, own)]))
-    planes, _ = lax.optimization_barrier((planes, after))
-    for c in range(2):
-        own = planes[c]
-        held = [own, lax.ppermute(own, "particle", middle),
-                lax.ppermute(own, "particle", inward), lax.ppermute(own, "particle", beyond)]
-
-        def find(need):
-            at = need // 2
-            which = jnp.where(at == z, 0, jnp.where(at == 3 - z, 1, jnp.where(at == plane, 2, 3)))
-            row = need % 2
-            return pick(which, [jnp.where(row == 0, h[0], h[1]) for h in held])
-
-        out = jnp.stack([find(jnp.where(z < 2, chosen[i], chosen[6 + i])) for i in range(2)])
-        sent = lax.ppermute(out, "particle", outward)
-        inner = (z == 1) | (z == 2)
-
-        def final(slot):
-            need = chosen[slot]
-            edge = jnp.where(need // 2 == z, jnp.where(need % 2 == 0, own[0], own[1]),
-                             jnp.where(slot % 2 == 0, sent[0], sent[1]))
-            return jnp.where(inner, find(need), edge)
-
-        mine = final(me)
-        got.append((mine, lax.ppermute(final(me ^ 1), "particle", swap)))
-    return got
+    return [lax.ppermute(planes, "particle", pairs) for pairs in (middle, inward, beyond)]
+
+
+def image_kernel(anc_ref, ord_ref, own_ref, mid_ref, in_ref, far_ref, q_ref, k_ref, v_ref,
+                 acc_ref, sum_ref, mine_ref, theirs_ref,
+                 outward, landed, give, came, send, recv, *, chunk, unit):
+    g, me, s = lax.axis_index("groups"), lax.axis_index("particle"), lax.axis_index("seq")
+    step = pl.program_id(0)
+    z, y = me // 2, me % 2
+    inner = jnp.logical_or(z == 1, z == 2)
+    edge = jnp.where(z < 2, 0, 3)
+    beside = jnp.where(z == 0, 1, jnp.where(z == 1, 0, jnp.where(z == 2, 3, 2)))
+    across = (g, 2 * z + 1 - y, s)
+    along = (g, 2 * beside + y, s)
+
+    def out_copy(c):
+        return pltpu.make_async_remote_copy(
+            src_ref=outward.at[c], dst_ref=landed.at[c], send_sem=send.at[c], recv_sem=recv.at[c],
+            device_id=along, device_id_type=MESH)
+
+    def swap_copy(c):
+        return pltpu.make_async_remote_copy(
+            src_ref=give.at[c], dst_ref=came.at[c], send_sem=send.at[2 + c],
+            recv_sem=recv.at[2 + c], device_id=across, device_id_type=MESH)
+
+    def find(c, need):
+        at, row = need // 2, need % 2
+        which = jnp.where(at == z, 0, jnp.where(at == 3 - z, 1, jnp.where(at == edge, 2, 3)))
+        res = own_ref[c, row]
+        for i, ref in enumerate((mid_ref, in_ref, far_ref), 1):
+            res = jnp.where(which == i, ref[c, row], res)
+        return res
+
+    need_mine = anc_ref[ord_ref[me]]
+    need_give = anc_ref[ord_ref[2 * z + 1 - y]]
+
+    def finish(c):
+        for ref, need, slot in ((mine_ref, need_mine, y), (give, need_give, 1 - y)):
+            ref[c] = jnp.where(need // 2 == z, own_ref[c, need % 2], landed[c, slot])
+        swap_copy(c).start()
+
+    @pl.when(step == 0)
+    def _():
+        greet([across, along])
+
+        @pl.when(inner)
+        def _():
+            for c in range(2):
+                for i in range(2):
+                    outward[c, i] = find(c, anc_ref[ord_ref[2 * edge + i]])
+                out_copy(c).start()
+            for c in range(2):
+                mine_ref[c] = find(c, need_mine)
+                give[c] = find(c, need_give)
+                swap_copy(c).start()
+
+    width = k_ref.shape[1]
+    vals = jnp.concatenate([v_ref[...], jnp.ones_like(v_ref)], axis=1)
+    for at in range(0, q_ref.shape[0], chunk):
+        r = slice(at, at + chunk)
+        sc = lax.dot_general(q_ref[r, :], k_ref[...], NT, preferred_element_type=F32)
+        p = jnp.exp2(sc * unit).astype(BF16)
+        o = jnp.dot(p, vals, preferred_element_type=F32)
+        acc_ref[r, :] = o[:, :width]
+        sum_ref[r, :] = o[:, width:]
+
+    last = pl.num_programs(0) - 1
+
+    @pl.when(jnp.logical_and(step == last - 1, jnp.logical_not(inner)))
+    def _():
+        out_copy(0).wait_recv()
+        finish(0)
+
+    @pl.when(step == last)
+    def _():
+        @pl.when(jnp.logical_not(inner))
+        def _():
+            out_copy(1).wait_recv()
+            finish(1)
+
+        @pl.when(inner)
+        def _():
+            for c in range(2):
+                out_copy(c).wait_send()
+
+        for c in range(2):
+            swap_copy(c).wait()
+            theirs_ref[c] = came[c]
+
+
+def image_attention(ancestors, order, own, others, q, k, v, width):
+    tokens, cols = q.shape
+    heads = cols // width
+    unit = LOG2E / width ** 0.5
+    out = jax.ShapeDtypeStruct((tokens, cols), F32)
+    two, _, rows, _ = own.shape
+    text = jax.ShapeDtypeStruct((two, rows, cols), BF16)
+    vmem = pl.BlockSpec(memory_space=pltpu.VMEM)
+    smem = pl.BlockSpec(memory_space=pltpu.SMEM)
+    head = pl.BlockSpec((tokens, width), lambda h: (0, h))
+    return pl.pallas_call(
+        functools.partial(image_kernel, chunk=256, unit=unit),
+        grid=(heads,),
+        in_specs=[smem, smem] + [vmem] * 4 + [head] * 3,
+        out_specs=[head, head, vmem, vmem],
+        out_shape=[out, out, text, text],
+        scratch_shapes=[pltpu.VMEM(own.shape, BF16), pltpu.VMEM(own.shape, BF16),
+                        pltpu.VMEM(text.shape, BF16), pltpu.VMEM(text.shape, BF16),
+                        pltpu.SemaphoreType.DMA((4,)), pltpu.SemaphoreType.DMA((4,))],
+        compiler_params=pltpu.CompilerParams(
+            collective_id=1, has_side_effects=True, vmem_limit_bytes=40 * 1024 * 1024),
+        cost_estimate=pl.CostEstimate(
+            flops=8 * tokens * tokens * cols, bytes_accessed=14 * tokens * cols,
+            transcendentals=tokens * tokens * heads),
+        name="image",
+    )(ancestors, order, own, *others, q, k, v)
 
 
 def body(latents, text_kv, ancestors, order, embed_weight, embed_bias, shift, scale,
          qkv_weight, norm_gains, *, particles):
     width = norm_gains.shape[1]
-    me = lax.axis_index("particle")
     seq = lax.axis_index("seq")
-    chosen = ancestors[order]
     lat = pack(latents[0].astype(BF16))
     kv = text_kv[0]
+    small = (embed_weight, embed_bias, shift, scale, norm_gains, qkv_weight)
     if particles == 8:
-        x_other, x_mine = route_latents(lat, chosen, me)
-        (ka, kb), (va, vb) = route_text(kv, chosen, me, x_mine)
+        x_other, x_mine, planes = gather(ancestors, order, lat, kv)
+        others = inward_planes(planes)
+        q, k, v = project(x_other, x_mine, *small)
+        acc, total, own, swapped = image_attention(ancestors, order, planes, others, q, k, v, width)
+        (ka, va), (kb, vb) = own, swapped
     else:
-        need = chosen[me]
+        need = ancestors[order][lax.axis_index("particle")]
         x_mine = lax.all_gather(lat, "particle", axis=0)[need]
         x_other = lax.ppermute(x_mine, "seq", [(0, 1), (1, 0)])
         text = lax.all_gather(kv, "particle", axis=0)[need]
         rows = text.shape[1] // 2
         ka, kb, va, vb = text[0, :rows], text[0, rows:], text[1, :rows], text[1, rows:]
-    q, k, v = project(x_other, x_mine, embed_weight, embed_bias, shift, scale, norm_gains, qkv_weight)
-    acc0, sum0 = image_attention(q, k, v, 0, width)
-    acc1, sum1 = image_attention(q, k, v, 1, width)
-    away = text_attention(q, ka, kb, va, vb, acc0, sum0, 0, width)
+        q, k, v = project(x_other, x_mine, *small)
+        acc, total = image_alone(q, k, v, width)
+    away = text_attention(q, ka, kb, va, vb, acc, total, 0, width)
     theirs = lax.ppermute(away, "seq", [(0, 1), (1, 0)])
-    mine = text_attention(q, ka, kb, va, vb, acc1, sum1, 1, width)
+    mine = text_attention(q, ka, kb, va, vb, acc, total, 1, width)
     left = jnp.where(seq == 0, mine, theirs)
     right = jnp.where(seq == 0, theirs, mine)
     return jnp.concatenate([left, right], axis=1)[None]

time: 118 us -> 107 us (0.907)
  Pallas kernels: 44.7 us -> 78 us
  starting transfers between devices: 30.2 us -> 9.51 us
  waiting for transfers between devices: 25.1 us -> 5.54 us
  between operations: 8.01 us -> 0.24 us
  local copies, waits for them, and re-layouts: 5.27 us -> 10.8 us
  other arithmetic: 4.45 us -> 2.6 us
    ppermute x18 -> x3, starting transfers between devices: 27.3 us -> 6.63 us  [inward_planes(): lax.ppermute(planes, 'particle', pairs)]
    ppermute x18 -> x3, waiting for transfers between devices: 25.1 us -> 5.54 us  [inward_planes(): lax.ppermute(planes, 'particle', pairs)]
    pallas_call x0 -> x1, Pallas kernels: none -> 18.3 us  [gather(): pl.pallas_call(gather_kernel, in_specs=[smem, smem, vmem, anyp], out_spec...]
    pallas_call x2 -> x1, Pallas kernels: 11.7 us -> 26 us  [image_attention(): pl.pallas_call(functools.partial(image_kernel, chunk=256, unit=unit), gri...]
    unnamed x23 -> x37, local copies, waits for them, and re-layouts: 3.96 us -> 10.7 us
    select_n x13 -> x0, other arithmetic: 1.62 us -> none  [the longest x1 0.66 us: body(): chosen = ancestors[order]]
  transfers between devices with their start and end apart: 19 -> 4, of which waited for: 7 -> 1; matrix products, arithmetic and copies ran while one was open for 3% -> 0% of each run, Pallas kernels for 35% -> 27%
where the time goes in v2:
time: 107 us
  Pallas kernels  78 us (73%)
  local copies, waits for them, and re-layouts  10.8 us (10%)
  starting transfers between devices  9.51 us (9%)
  waiting for transfers between devices  5.54 us (5%)
  other arithmetic  2.6 us (2%)
    pallas_call x1, Pallas kernels, image_attention(): pl.pallas_call(functools.partial(image_kernel, chunk=256, unit=unit), gri...  26 us
    pallas_call x1, Pallas kernels, project(): pl.pallas_call(functools.partial(project_kernel, chunk=min(128, x0.shape[...  25.6 us
    pallas_call x1, Pallas kernels, gather(): pl.pallas_call(gather_kernel, in_specs=[smem, smem, vmem, anyp], out_spec...  18.3 us
    unnamed x37, local copies, waits for them, and re-layouts  10.7 us
    pallas_call x2, Pallas kernels, text_attention(): pl.pallas_call(functools.partial(text_kernel, unit=unit), grid=(heads,),...  8.05 us
    ppermute x3, starting transfers between devices, inward_planes(): lax.ppermute(planes, 'particle', pairs)  6.63 us
    ppermute x3, waiting for transfers between devices, inward_planes(): lax.ppermute(planes, 'particle', pairs)  5.54 us
    ppermute x1, starting transfers between devices, body(): theirs = lax.ppermute(away, 'seq', [(0, 1), (1, 0)])  2.88 us
  transfers between devices with their start and end apart: 4, of which 1 were waited for; matrix products, arithmetic and copies ran while one was open for 0% of the time, Pallas kernels for 27%

profile of v2, /device:TPU:1, one launch (start us, length us, event | category | flops | bytes accessed | tf_op | source)
XLA Modules:
  0.0 106.7 jit_solution(1766854061780021994)
XLA Ops:
  0.0 1.1 %copy.11 = bf16[1,512,64]{2,1,0:T(8,128)(2,1)S(1)} copy(f32[1,512,64]{1,2,0:T(8,128)} %param.10) | data formatting | bytes 196608 | tf_op args[0]
  1.1 0.1 pad_maximum_fusion.lat_ref
  1.2 0.0 copy-start.8
  1.2 1.1 %copy-done.8 = bf16[1,2,256,768]{3,2,1,0:T(8,128)(2,1)S(1)} copy-done((bf16[1,2,256,768]{3,2,1,0:T(8,128)(2,1)S(1)}, bf16[1,2,256,768]{3,2,1,0:T(8,128)(2,1)}, u32[]{:S(2)}) %copy-start.8) | copy-done | bytes 786456
  2.4 0.7 copy-done.9
  3.0 0.7 copy-done.11
  3.7 18.3 %gather.1 = (bf16[256,128]{1,0:T(8,128)(2,1)S(1)}, bf16[256,128]{1,0:T(8,128)(2,1)S(1)}, bf16[2,2,128,768]{3,2,1,0:T(8,128)(2,1)S(1)}) custom-call(s32[8]{0:T(128)S(1)} %copy-done.9, s32[8]{0:T(128)S(1)} %copy-done.11, bf16[256,128]{1,0:T(8,128)(2,1)S(1)} %pad_maximum_fusion.lat_ref, bf16[2,256,768]{2,1,0:T(8,128)(2,1)S(1)} %bitcast.18), custom_call_target="tpu_custom_call" | custom-call | bytes 20000000 | tf_op jit(solution)/shard_map/gather/pallas_call | solution.py:210
  22.0 0.7 collective-permute-start
  22.7 3.7 %collective-permute-start.1 = (bf16[2,2,128,768]{3,2,1,0:T(8,128)(2,1)S(1)}, bf16[2,2,128,768]{3,2,1,0:T(8,128)(2,1)S(1)}, u32[]{:S(2)}, u32[]{:S(2)}) collective-permute-start(bf16[2,2,128,768]{3,2,1,0:T(8,128)(2,1)S(1)} %get-tuple-element.18.own_ref), channel_id=1, source_target_pairs={{0,4},{2,6},{12,8},{14,10},{1,5},{3,7},{13,9},{15,11},{16,20},{18,... | collective-permute-start | bytes 2359304 | tf_op jit(solution)/shard_map/ppermute | solution.py:230
  26.4 2.2 %collective-permute-start.2 = (bf16[2,2,128,768]{3,2,1,0:T(8,128)(2,1)S(1)}, bf16[2,2,128,768]{3,2,1,0:T(8,128)(2,1)S(1)}, u32[]{:S(2)}, u32[]{:S(2)}) collective-permute-start(bf16[2,2,128,768]{3,2,1,0:T(8,128)(2,1)S(1)} %get-tuple-element.18.own_ref), channel_id=1, source_target_pairs={{0,8},{2,10},{12,4},{14,6},{1,9},{3,11},{13,5},{15,7},{16,24},{18,... | collective-permute-start | bytes 2359304 | tf_op jit(solution)/shard_map/ppermute | solution.py:230
  28.7 0.0 copy-start.10
  28.7 0.0 copy-start.12
  28.7 25.6 %project.1 = (bf16[1024,768]{1,0:T(8,128)(2,1)S(1)}, bf16[1024,768]{1,0:T(8,128)(2,1)S(1)}, bf16[1024,768]{1,0:T(8,128)(2,1)S(1)}) custom-call(bf16[256,128]{1,0:T(8,128)(2,1)S(1)} %get-tuple-element.15.x0_ref, bf16[256,128]{1,0:T(8,128)(2,1)S(1)} %get-tuple-element.16.x1_ref, bf16[64,3072]{1,0:T(8,128)(2,1)S(1)} %copy-done.13, f32[1,3072]{1,0:T(1,128)S(1)} %bitcast.19, ...), custom_call_target="tpu_custom_call" | custom-call | flops 14495514624 | bytes 18874368 | tf_op jit(solution)/shard_map/project/pallas_call | solution.py:65
  54.3 0.0 copy-start.2
  54.3 0.0 collective-permute-done.mid_ref
  54.3 0.0 collective-permute-done.1.in_ref
  54.4 5.5 %collective-permute-done.2.far_ref = bf16[2,2,128,768]{3,2,1,0:T(8,128)(2,1)S(1)} collective-permute-done((bf16[2,2,128,768]{3,2,1,0:T(8,128)(2,1)S(1)}, bf16[2,2,128,768]{3,2,1,0:T(8,128)(2,1)S(1)}, u32[]{:S(2)}, u32[]{:S(2)}) %collective-permute-start.2) | collective-permute-done | bytes 786464 | tf_op jit(solution)/shard_map/ppermute | solution.py:230
  59.9 0.0 copy-done.12
  59.9 26.0 %image.1 = (f32[1024,768]{1,0:T(8,128)S(1)}, f32[1024,768]{1,0:T(8,128)}, bf16[2,128,768]{2,1,0:T(8,128)(2,1)S(1)}, bf16[2,128,768]{2,1,0:T(8,128)(2,1)S(1)}) custom-call(s32[8]{0:T(128)S(1)} %copy-done.10, s32[8]{0:T(128)S(1)} %copy-done.12, bf16[2,2,128,768]{3,2,1,0:T(8,128)(2,1)S(1)} %get-tuple-element.18.own_ref, ...), custom_call_target="tpu_custom_call" | custom-call | flops 6442450944 | bytes 11010048 | tf_op jit(solution)/shard_map/image/pallas_call | solution.py:330
  85.9 0.1 slice_bitcast_fusion
  86.0 2.0 %copy-done = f32[1024,768]{1,0:T(8,128)S(1)} copy-done((f32[1024,768]{1,0:T(8,128)S(1)}, f32[1024,768]{1,0:T(8,128)}, u32[]{:S(2)}) %copy-start) | copy-done | bytes 3145752
  88.0 4.4 %text_0.1 = bf16[512,768]{1,0:T(8,128)(2,1)} custom-call(bf16[1024,768]{1,0:T(8,128)(2,1)S(1)} %get-tuple-element.17.q_ref, bf16[128,768]{1,0:T(8,128)(2,1)S(1)} %get-tuple-element.33.ka_ref, bf16[128,768]{1,0:T(8,128)(2,1)S(1)} %get-tuple-element.28.kb_ref, bf16[128,768]{1,0:T(8,128)(2,1)S(1)} %get-tuple-element.34.va_ref, ...), custom_call_target="tpu_custom_call" | custom-call | flops 805306368 | bytes 5505024 | tf_op jit(solution)/shard_map/text_0/pallas_call | solution.py:129
  92.4 0.0 copy-done.4
  92.4 2.9 %collective-permute-start.3 = (bf16[512,768]{1,0:T(8,128)(2,1)}, bf16[512,768]{1,0:T(8,128)(2,1)}, u32[]{:S(2)}, u32[]{:S(2)}) collective-permute-start(bf16[512,768]{1,0:T(8,128)(2,1)} %text_0.1), channel_id=1, source_target_pairs={{0,1},{1,0},{2,3},{3,2},{4,5},{5,4},{6,7},{7,6},{8,9},{9,8},{10,11... | collective-permute-start | bytes 2359304 | tf_op jit(solution)/shard_map/ppermute | solution.py:371
  95.3 1.9 %copy-done.1 = f32[1024,768]{1,0:T(8,128)S(1)} copy-done((f32[1024,768]{1,0:T(8,128)S(1)}, f32[1024,768]{1,0:T(8,128)}, u32[]{:S(2)}) %copy-start.1) | copy-done | bytes 3145752
  97.2 1.4 %copy-done.3 = bf16[1024,768]{1,0:T(8,128)(2,1)S(1)} copy-done((bf16[1024,768]{1,0:T(8,128)(2,1)S(1)}, bf16[1024,768]{1,0:T(8,128)(2,1)}, u32[]{:S(2)}) %copy-start.3) | copy-done | bytes 1572888
  98.6 0.9 copy-done.5
  99.5 0.9 copy-done.7
  100.5 3.7 %text_1.1 = bf16[512,768]{1,0:T(8,128)(2,1)S(1)} custom-call(bf16[1024,768]{1,0:T(8,128)(2,1)S(1)} %copy-done.3, bf16[128,768]{1,0:T(8,128)(2,1)S(1)} %copy-done.5, bf16[128,768]{1,0:T(8,128)(2,1)S(1)} %get-tuple-element.28.kb_ref, bf16[128,768]{1,0:T(8,128)(2,1)S(1)} %copy-done.7, bf16[128,768]{1,0:T(8,128)(2,1)S(1)} %get-tuple-element.27.vb_ref, ...), custom_call_target="tpu_custom_call" | custom-call | flops 805306368 | bytes 5505024 | tf_op jit(solution)/shard_map/text_1/pallas_call | solution.py:129
  104.1 0.0 collective-permute-done.3
  104.2 1.2 %broadcast_select_fusion.1 = (bf16[512,768]{1,0:T(8,128)(2,1)S(1)}, bf16[512,768]{1,0:T(8,128)(2,1)S(1)}) fusion(bf16[512,768]{1,0:T(8,128)(2,1)S(1)} %text_1.1, bf16[512,768]{1,0:T(8,128)(2,1)} %collective-permute-done.3, pred[]{:T(512)S(6)} %eq.4), kind=kLoop, calls=%fused_computation.2 | loop fusion | flops 786432 | bytes 3145729 | tf_op jit(solution)/shard_map/jit(_where)/select_n | solution.py:373
  105.4 1.3 %maximum_bitcast_fusion = bf16[1,512,1536]{2,1,0:T(8,128)(2,1)} fusion(bf16[512,768]{1,0:T(8,128)(2,1)S(1)} %get-tuple-element.26, bf16[512,768]{1,0:T(8,128)(2,1)S(1)} %get-tuple-element.25), kind=kLoop, calls=%fused_computation | loop fusion | flops 3145728 | bytes 3145728 | tf_op jit(solution)/shard_map/broadcast_in_dim | solution.py:375
  (23 shorter events, 0.1 us)
Async XLA Ops:
  0.0 28.6 %copy-start.14 = (f32[3072]{0:T(1024)S(1)}, f32[3072]{0:T(1024)}, u32[]{:S(2)}) copy-start(f32[3072]{0:T(1024)} %param.15) | copy-start | bytes 36868
  0.0 28.6 %copy-start.15 = (f32[3072]{0:T(1024)S(1)}, f32[3072]{0:T(1024)}, u32[]{:S(2)}) copy-start(f32[3072]{0:T(1024)} %param.16) | copy-start | bytes 36868
  0.0 28.6 %copy-start.16 = (f32[3072]{0:T(1024)S(1)}, f32[3072]{0:T(1024)}, u32[]{:S(2)}) copy-start(f32[3072]{0:T(1024)} %param.17) | copy-start | bytes 36868
  0.0 28.7 %copy-start.13 = (bf16[64,3072]{1,0:T(8,128)(2,1)S(1)}, bf16[64,3072]{1,0:T(8,128)(2,1)}, u32[]{:S(2)}) copy-start(bf16[64,3072]{1,0:T(8,128)(2,1)} %ew_ref.1) | copy-start | bytes 1179652
  0.0 28.7 %copy-start.17 = (f32[2,128]{1,0:T(2,128)S(1)}, f32[2,128]{1,0:T(2,128)}, u32[]{:S(2)}) copy-start(f32[2,128]{1,0:T(2,128)} %gain_ref.1) | copy-start | bytes 3076
  1.2 1.1 %copy-start.8 = (bf16[1,2,256,768]{3,2,1,0:T(8,128)(2,1)S(1)}, bf16[1,2,256,768]{3,2,1,0:T(8,128)(2,1)}, u32[]{:S(2)}) copy-start(bf16[1,2,256,768]{3,2,1,0:T(8,128)(2,1)} %param.11) | copy-start | bytes 2359300
  2.4 0.7 copy-start.9
  3.0 0.7 copy-start.11
  22.0 32.4 %collective-permute-start = (bf16[2,2,128,768]{3,2,1,0:T(8,128)(2,1)S(1)}, bf16[2,2,128,768]{3,2,1,0:T(8,128)(2,1)S(1)}, u32[]{:S(2)}, u32[]{:S(2)}) collective-permute-start(bf16[2,2,128,768]{3,2,1,0:T(8,128)(2,1)S(1)} %get-tuple-element.18.own_ref), channel_id=1, source_target_pairs={{4,8},{6,10},{8,4},{10,6},{5,9},{7,11},{9,5},{11,7},{20,24},{22,26... | collective-permute-start | bytes 2359304 | tf_op jit(solution)/shard_map/ppermute | solution.py:230
  22.7 31.7 %collective-permute-start.1 = (bf16[2,2,128,768]{3,2,1,0:T(8,128)(2,1)S(1)}, bf16[2,2,128,768]{3,2,1,0:T(8,128)(2,1)S(1)}, u32[]{:S(2)}, u32[]{:S(2)}) collective-permute-start(bf16[2,2,128,768]{3,2,1,0:T(8,128)(2,1)S(1)} %get-tuple-element.18.own_ref), channel_id=1, source_target_pairs={{0,4},{2,6},{12,8},{14,10},{1,5},{3,7},{13,9},{15,11},{16,20},{18,... | collective-permute-start | bytes 2359304 | tf_op jit(solution)/shard_map/ppermute | solution.py:230
  26.4 33.5 %collective-permute-start.2 = (bf16[2,2,128,768]{3,2,1,0:T(8,128)(2,1)S(1)}, bf16[2,2,128,768]{3,2,1,0:T(8,128)(2,1)S(1)}, u32[]{:S(2)}, u32[]{:S(2)}) collective-permute-start(bf16[2,2,128,768]{3,2,1,0:T(8,128)(2,1)S(1)} %get-tuple-element.18.own_ref), channel_id=1, source_target_pairs={{0,8},{2,10},{12,4},{14,6},{1,9},{3,11},{13,5},{15,7},{16,24},{18,... | collective-permute-start | bytes 2359304 | tf_op jit(solution)/shard_map/ppermute | solution.py:230
  28.7 31.2 %copy-start.10 = (s32[8]{0:T(128)S(1)}, s32[8]{0:T(128)}, u32[]{:S(2)}) copy-start(s32[8]{0:T(128)} %anc_ref.3) | copy-start | bytes 100
  28.7 31.2 %copy-start.12 = (s32[8]{0:T(128)S(1)}, s32[8]{0:T(128)}, u32[]{:S(2)}) copy-start(s32[8]{0:T(128)} %ord_ref.3) | copy-start | bytes 100
  54.3 31.7 %copy-start.2 = (bf16[1024,768]{1,0:T(8,128)(2,1)}, bf16[1024,768]{1,0:T(8,128)(2,1)S(1)}, u32[]{:S(2)}) copy-start(bf16[1024,768]{1,0:T(8,128)(2,1)S(1)} %get-tuple-element.17.q_ref) | copy-start | bytes 4718596
  86.0 6.4 %copy-start.4 = (bf16[128,768]{1,0:T(8,128)(2,1)}, bf16[128,768]{1,0:T(8,128)(2,1)S(1)}, u32[]{:S(2)}) copy-start(bf16[128,768]{1,0:T(8,128)(2,1)S(1)} %get-tuple-element.33.ka_ref) | copy-start | bytes 589828
  86.0 6.4 %copy-start.6 = (bf16[128,768]{1,0:T(8,128)(2,1)}, bf16[128,768]{1,0:T(8,128)(2,1)S(1)}, u32[]{:S(2)}) copy-start(bf16[128,768]{1,0:T(8,128)(2,1)S(1)} %get-tuple-element.34.va_ref) | copy-start | bytes 589828
  86.0 2.0 %copy-start = (f32[1024,768]{1,0:T(8,128)S(1)}, f32[1024,768]{1,0:T(8,128)}, u32[]{:S(2)}) copy-start(f32[1024,768]{1,0:T(8,128)} %get-tuple-element.24.sum_ref) | copy-start | bytes 9437188
  92.4 11.7 %collective-permute-start.3 = (bf16[512,768]{1,0:T(8,128)(2,1)}, bf16[512,768]{1,0:T(8,128)(2,1)}, u32[]{:S(2)}, u32[]{:S(2)}) collective-permute-start(bf16[512,768]{1,0:T(8,128)(2,1)} %text_0.1), channel_id=1, source_target_pairs={{0,1},{1,0},{2,3},{3,2},{4,5},{5,4},{6,7},{7,6},{8,9},{9,8},{10,11... | collective-permute-start | bytes 2359304 | tf_op jit(solution)/shard_map/ppermute | solution.py:371
  95.3 1.9 %copy-start.1 = (f32[1024,768]{1,0:T(8,128)S(1)}, f32[1024,768]{1,0:T(8,128)}, u32[]{:S(2)}) copy-start(f32[1024,768]{1,0:T(8,128)} %get-tuple-element.24.sum_ref) | copy-start | bytes 9437188
  97.2 1.4 %copy-start.3 = (bf16[1024,768]{1,0:T(8,128)(2,1)S(1)}, bf16[1024,768]{1,0:T(8,128)(2,1)}, u32[]{:S(2)}) copy-start(bf16[1024,768]{1,0:T(8,128)(2,1)} %copy-done.2) | copy-start | bytes 4718596
  98.6 0.9 copy-start.5
  99.5 0.9 copy-start.7

commit v3 on v2

--- a/solution.py
+++ b/solution.py
@@ -52,7 +52,7 @@
             v_ref[r, c] = mixed[:, base + 2 * width:base + 3 * width].astype(BF16)
 
 
-def project(x0, x1, embed_weight, embed_bias, shift, scale, gains, weight):
+def project(x0, x1, embed_weight, embed_bias, shift, scale, gains, weight, route=None):
     d, cols = weight.shape
     width = gains.shape[1]
     heads = cols // (3 * width)
@@ -62,20 +62,44 @@
     small = (x0, x1, embed_weight, embed_bias[None], shift[None], scale[None], gains)
     out = jax.ShapeDtypeStruct((rows, heads * width), BF16)
     ospec = pl.BlockSpec((rows, per * width), lambda j: (0, j))
+    cost = pl.CostEstimate(
+        flops=2 * rows * d * cols, bytes_accessed=2 * d * cols + 6 * rows * heads * width,
+        transcendentals=0)
+    chunk = min(128, x0.shape[0])
+    in_specs = [whole(a) for a in small] + [pl.BlockSpec((d, per * 3 * width), lambda j: (0, j))]
+    scratch = [pltpu.VMEM((rows, d), BF16)]
+    if route is None:
+        return pl.pallas_call(
+            functools.partial(project_kernel, chunk=chunk, width=width),
+            grid=(heads // per,),
+            in_specs=in_specs,
+            out_specs=[ospec] * 3,
+            out_shape=[out] * 3,
+            scratch_shapes=scratch,
+            compiler_params=pltpu.CompilerParams(vmem_limit_bytes=44 * 1024 * 1024),
+            cost_estimate=cost,
+            name="project",
+        )(*small, weight)
+    own = route[2]
+    vmem = pl.BlockSpec(memory_space=pltpu.VMEM)
+    smem = pl.BlockSpec(memory_space=pltpu.SMEM)
+    three = (3,) + own.shape
+    half = own.shape[1:]
     return pl.pallas_call(
-        functools.partial(project_kernel, chunk=min(128, x0.shape[0]), width=width),
+        functools.partial(routed_kernel, chunk=chunk, width=width),
         grid=(heads // per,),
-        in_specs=[whole(a) for a in small]
-        + [pl.BlockSpec((d, per * 3 * width), lambda j: (0, j))],
-        out_specs=[ospec] * 3,
-        out_shape=[out] * 3,
-        scratch_shapes=[pltpu.VMEM((rows, d), BF16)],
-        compiler_params=pltpu.CompilerParams(vmem_limit_bytes=44 * 1024 * 1024),
-        cost_estimate=pl.CostEstimate(
-            flops=2 * rows * d * cols, bytes_accessed=2 * d * cols + 6 * rows * heads * width,
-            transcendentals=0),
-        name="project",
-    )(*small, weight)
+        in_specs=[smem, smem, vmem] + in_specs,
+        out_specs=[ospec] * 3 + [vmem] * 2,
+        out_shape=[out] * 3 + [jax.ShapeDtypeStruct(three, BF16), jax.ShapeDtypeStruct(half, BF16)],
+        scratch_shapes=scratch + [
+            pltpu.VMEM((3,) + half, BF16), pltpu.VMEM((3,) + half, BF16),
+            pltpu.VMEM(half, BF16), pltpu.VMEM(half, BF16),
+            pltpu.SemaphoreType.DMA((7,)), pltpu.SemaphoreType.DMA((7,))],
+        compiler_params=pltpu.CompilerParams(
+            collective_id=2, has_side_effects=True, vmem_limit_bytes=58 * 1024 * 1024),
+        cost_estimate=cost,
+        name="project_routed",
+    )(*route, *small, weight)
 
 
 def image_alone_kernel(q_ref, k_ref, v_ref, acc_ref, sum_ref, *, chunk, unit):
@@ -100,7 +124,7 @@
         in_specs=[head] * 3,
         out_specs=[head] * 2,
         out_shape=[out] * 2,
-        compiler_params=pltpu.CompilerParams(vmem_limit_bytes=32 * 1024 * 1024),
+        compiler_params=pltpu.CompilerParams(vmem_limit_bytes=58 * 1024 * 1024),
         name="image_alone",
     )(q, k, v)
 
@@ -133,7 +157,7 @@
         + [pl.BlockSpec((rows, width), lambda h: (half, h))] * 2,
         out_specs=full,
         out_shape=jax.ShapeDtypeStruct((rows, cols), BF16),
-        compiler_params=pltpu.CompilerParams(vmem_limit_bytes=32 * 1024 * 1024),
+        compiler_params=pltpu.CompilerParams(vmem_limit_bytes=58 * 1024 * 1024),
         cost_estimate=pl.CostEstimate(
             flops=16 * rows * ka.shape[0] * cols, bytes_accessed=14 * rows * cols,
             transcendentals=2 * rows * ka.shape[0] * heads),
@@ -217,20 +241,96 @@
                         pltpu.SemaphoreType.DMA((7,)), pltpu.SemaphoreType.DMA((7,)),
                         pltpu.SemaphoreType.DMA],
         compiler_params=pltpu.CompilerParams(
-            collective_id=0, has_side_effects=True, vmem_limit_bytes=16 * 1024 * 1024),
+            collective_id=0, has_side_effects=True, vmem_limit_bytes=58 * 1024 * 1024),
         cost_estimate=pl.CostEstimate(flops=0, bytes_accessed=20000000, transcendentals=0),
         name="gather",
     )(ancestors, order, lat, kv)
 
 
-def inward_planes(planes):
-    middle = [(2, 4), (3, 5), (4, 2), (5, 3)]
-    inward = [(0, 2), (1, 3), (6, 4), (7, 5)]
-    beyond = [(0, 4), (1, 5), (6, 2), (7, 3)]
-    return [lax.ppermute(planes, "particle", pairs) for pairs in (middle, inward, beyond)]
-
-
-def image_kernel(anc_ref, ord_ref, own_ref, mid_ref, in_ref, far_ref, q_ref, k_ref, v_ref,
+def choose(own, others, z, edge, need, c):
+    at, row = need // 2, need % 2
+    which = jnp.where(at == z, 0, jnp.where(at == 3 - z, 1, jnp.where(at == edge, 2, 3)))
+    res = own[c, row]
+    for i in range(3):
+        res = jnp.where(which == i + 1, others(i, c, row), res)
+    return res
+
+
+def routed_kernel(anc_ref, ord_ref, own_ref, x0_ref, x1_ref, ew_ref, eb_ref, sh_ref, sc_ref,
+                  gain_ref, w_ref, q_ref, k_ref, v_ref, others_ref, keys_ref,
+                  normed, got_keys, got_vals, outward, landed, send, recv, *, chunk, width):
+    g, me, s = lax.axis_index("groups"), lax.axis_index("particle"), lax.axis_index("seq")
+    step = pl.program_id(0)
+    last = pl.num_programs(0) - 1
+    z, y = me // 2, me % 2
+    inner = jnp.logical_or(z == 1, z == 2)
+    outer = jnp.logical_not(inner)
+    edge = jnp.where(z < 2, 0, 3)
+    beside = jnp.where(z == 0, 1, jnp.where(z == 1, 0, jnp.where(z == 2, 3, 2)))
+
+    def at(plane):
+        return (g, 2 * plane + y, s)
+
+    targets = (3 - z, beside, 3 - beside)
+
+    def plane_copy(kind, c):
+        return pltpu.make_async_remote_copy(
+            src_ref=own_ref.at[c], dst_ref=(got_keys, got_vals)[c].at[kind], send_sem=send.at[2 * kind + c],
+            recv_sem=recv.at[2 * kind + c], device_id=at(targets[kind]), device_id_type=MESH)
+
+    key_copy = pltpu.make_async_remote_copy(
+        src_ref=outward, dst_ref=landed, send_sem=send.at[6], recv_sem=recv.at[6],
+        device_id=at(beside), device_id_type=MESH)
+
+    @pl.when(step == 0)
+    def _():
+        greet([at((z + k) % 4) for k in (1, 2, 3)])
+
+        @pl.when(inner)
+        def _():
+            for c in range(2):
+                plane_copy(0, c).start()
+
+        @pl.when(outer)
+        def _():
+            for c in range(2):
+                plane_copy(2, c).start()
+                plane_copy(1, c).start()
+
+    @pl.when(jnp.logical_and(step == last, inner))
+    def _():
+        for kind in range(3):
+            plane_copy(kind, 0).wait_recv()
+        for i in range(2):
+            outward[i] = choose(
+                own_ref, lambda i, c, row: got_keys[i, row], z, edge, anc_ref[ord_ref[2 * edge + i]], 0)
+        key_copy.start()
+
+    project_kernel(x0_ref, x1_ref, ew_ref, eb_ref, sh_ref, sc_ref, gain_ref, w_ref,
+                   q_ref, k_ref, v_ref, normed, chunk=chunk, width=width)
+
+    @pl.when(step == last)
+    def _():
+        @pl.when(inner)
+        def _():
+            for kind in range(3):
+                plane_copy(kind, 1).wait_recv()
+            others_ref[:, 0] = got_keys[...]
+            others_ref[:, 1] = got_vals[...]
+            for c in range(2):
+                plane_copy(0, c).wait_send()
+            key_copy.wait_send()
+
+        @pl.when(outer)
+        def _():
+            for c in range(2):
+                plane_copy(2, c).wait_send()
+                plane_copy(1, c).wait_send()
+            key_copy.wait_recv()
+            keys_ref[...] = landed[...]
+
+
+def image_kernel(anc_ref, ord_ref, own_ref, others_ref, keys_ref, q_ref, k_ref, v_ref,
                  acc_ref, sum_ref, mine_ref, theirs_ref,
                  outward, landed, give, came, send, recv, *, chunk, unit):
     g, me, s = lax.axis_index("groups"), lax.axis_index("particle"), lax.axis_index("seq")
@@ -242,30 +342,24 @@
     across = (g, 2 * z + 1 - y, s)
     along = (g, 2 * beside + y, s)
 
-    def out_copy(c):
-        return pltpu.make_async_remote_copy(
-            src_ref=outward.at[c], dst_ref=landed.at[c], send_sem=send.at[c], recv_sem=recv.at[c],
-            device_id=along, device_id_type=MESH)
+    out_copy = pltpu.make_async_remote_copy(
+        src_ref=outward, dst_ref=landed, send_sem=send.at[0], recv_sem=recv.at[0],
+        device_id=along, device_id_type=MESH)
 
     def swap_copy(c):
         return pltpu.make_async_remote_copy(
-            src_ref=give.at[c], dst_ref=came.at[c], send_sem=send.at[2 + c],
-            recv_sem=recv.at[2 + c], device_id=across, device_id_type=MESH)
+            src_ref=give.at[c], dst_ref=came.at[c], send_sem=send.at[1 + c],
+            recv_sem=recv.at[1 + c], device_id=across, device_id_type=MESH)
 
     def find(c, need):
-        at, row = need // 2, need % 2
-        which = jnp.where(at == z, 0, jnp.where(at == 3 - z, 1, jnp.where(at == edge, 2, 3)))
-        res = own_ref[c, row]
-        for i, ref in enumerate((mid_ref, in_ref, far_ref), 1):
-            res = jnp.where(which == i, ref[c, row], res)
-        return res
+        return choose(own_ref, lambda i, c, row: others_ref[i, c, row], z, edge, need, c)
 
     need_mine = anc_ref[ord_ref[me]]
     need_give = anc_ref[ord_ref[2 * z + 1 - y]]
 
-    def finish(c):
+    def finish(c, far):
         for ref, need, slot in ((mine_ref, need_mine, y), (give, need_give, 1 - y)):
-            ref[c] = jnp.where(need // 2 == z, own_ref[c, need % 2], landed[c, slot])
+            ref[c] = jnp.where(need // 2 == z, own_ref[c, need % 2], far[slot])
         swap_copy(c).start()
 
     @pl.when(step == 0)
@@ -274,14 +368,17 @@
 
         @pl.when(inner)
         def _():
-            for c in range(2):
-                for i in range(2):
-                    outward[c, i] = find(c, anc_ref[ord_ref[2 * edge + i]])
-                out_copy(c).start()
+            for i in range(2):
+                outward[i] = find(1, anc_ref[ord_ref[2 * edge + i]])
+            out_copy.start()
             for c in range(2):
                 mine_ref[c] = find(c, need_mine)
                 give[c] = find(c, need_give)
                 swap_copy(c).start()
+
+        @pl.when(jnp.logical_not(inner))
+        def _():
+            finish(0, keys_ref)
 
     width = k_ref.shape[1]
     vals = jnp.concatenate([v_ref[...], jnp.ones_like(v_ref)], axis=1)
@@ -297,27 +394,21 @@
 
     @pl.when(jnp.logical_and(step == last - 1, jnp.logical_not(inner)))
     def _():
-        out_copy(0).wait_recv()
-        finish(0)
+        out_copy.wait_recv()
+        finish(1, landed)
 
     @pl.when(step == last)
     def _():
-        @pl.when(jnp.logical_not(inner))
-        def _():
-            out_copy(1).wait_recv()
-            finish(1)
-
         @pl.when(inner)
         def _():
-            for c in range(2):
-                out_copy(c).wait_send()
+            out_copy.wait_send()
 
         for c in range(2):
             swap_copy(c).wait()
             theirs_ref[c] = came[c]
 
 
-def image_attention(ancestors, order, own, others, q, k, v, width):
+def image_attention(ancestors, order, own, others, keys, q, k, v, width):
     tokens, cols = q.shape
     heads = cols // width
     unit = LOG2E / width ** 0.5
@@ -330,19 +421,19 @@
     return pl.pallas_call(
         functools.partial(image_kernel, chunk=256, unit=unit),
         grid=(heads,),
-        in_specs=[smem, smem] + [vmem] * 4 + [head] * 3,
+        in_specs=[smem, smem] + [vmem] * 3 + [head] * 3,
         out_specs=[head, head, vmem, vmem],
         out_shape=[out, out, text, text],
-        scratch_shapes=[pltpu.VMEM(own.shape, BF16), pltpu.VMEM(own.shape, BF16),
+        scratch_shapes=[pltpu.VMEM(own.shape[1:], BF16), pltpu.VMEM(own.shape[1:], BF16),
                         pltpu.VMEM(text.shape, BF16), pltpu.VMEM(text.shape, BF16),
-                        pltpu.SemaphoreType.DMA((4,)), pltpu.SemaphoreType.DMA((4,))],
+                        pltpu.SemaphoreType.DMA((3,)), pltpu.SemaphoreType.DMA((3,))],
         compiler_params=pltpu.CompilerParams(
-            collective_id=1, has_side_effects=True, vmem_limit_bytes=40 * 1024 * 1024),
+            collective_id=1, has_side_effects=True, vmem_limit_bytes=58 * 1024 * 1024),
         cost_estimate=pl.CostEstimate(
             flops=8 * tokens * tokens * cols, bytes_accessed=14 * tokens * cols,
             transcendentals=tokens * tokens * heads),
         name="image",
-    )(ancestors, order, own, *others, q, k, v)
+    )(ancestors, order, own, others, keys, q, k, v)
 
 
 def body(latents, text_kv, ancestors, order, embed_weight, embed_bias, shift, scale,
@@ -354,9 +445,9 @@
     small = (embed_weight, embed_bias, shift, scale, norm_gains, qkv_weight)
     if particles == 8:
         x_other, x_mine, planes = gather(ancestors, order, lat, kv)
-        others = inward_planes(planes)
-        q, k, v = project(x_other, x_mine, *small)
-        acc, total, own, swapped = image_attention(ancestors, order, planes, others, q, k, v, width)
+        q, k, v, others, keys = project(x_other, x_mine, *small, route=(ancestors, order, planes))
+        acc, total, own, swapped = image_attention(
+            ancestors, order, planes, others, keys, q, k, v, width)
         (ka, va), (kb, vb) = own, swapped
     else:
         need = ancestors[order][lax.axis_index("particle")]

time: 107 us -> 101 us (0.944)
  Pallas kernels: 78 us -> 91 us
  local copies, waits for them, and re-layouts: 10.8 us -> 3.15 us
  starting transfers between devices: 9.51 us -> 2.98 us
  waiting for transfers between devices: 5.54 us -> 0.01 us
    pallas_call x1, Pallas kernels: 25.6 us -> 39.9 us  [project(): pl.pallas_call(functools.partial(routed_kernel, chunk=chunk, width=width)...]
    unnamed x37 -> x1, local copies, waits for them, and re-layouts: 10.7 us -> 1.02 us
    pallas_call x1, Pallas kernels: 26 us -> 18.7 us  [image_attention(): pl.pallas_call(functools.partial(image_kernel, chunk=256, unit=unit), gri...]
    ppermute x3 -> x0, starting transfers between devices: 6.63 us -> none  [inward_planes(): lax.ppermute(planes, 'particle', pairs)]
    ppermute x3 -> x0, waiting for transfers between devices: 5.54 us -> none  [inward_planes(): lax.ppermute(planes, 'particle', pairs)]
    pallas_call x2, Pallas kernels: 8.05 us -> 12.9 us  [text_attention(): pl.pallas_call(functools.partial(text_kernel, unit=unit), grid=(heads,),...]
    another operation x1, local copies, waits for them, and re-layouts: 0.05 us -> 2.12 us  [body(): (ka, va), (kb, vb) = (own, swapped)]
    pallas_call x1, Pallas kernels: 18.3 us -> 19.5 us  [gather(): pl.pallas_call(gather_kernel, in_specs=[smem, smem, vmem, anyp], out_spec...]
  transfers between devices with their start and end apart: 4 -> 1, of which waited for: 1 -> 0; matrix products, arithmetic and copies ran while one was open for 0% -> 0% of each run, Pallas kernels for 27% -> 6%
where the time goes in v3:
time: 101 us; the launch traced here: 100 us
  Pallas kernels  91 us (90%)
  other arithmetic  3.22 us (3%)
  local copies, waits for them, and re-layouts  3.15 us (3%)
  starting transfers between devices  2.98 us (3%)
    pallas_call x1, Pallas kernels, project(): pl.pallas_call(functools.partial(routed_kernel, chunk=chunk, width=width)...  39.9 us
    pallas_call x1, Pallas kernels, gather(): pl.pallas_call(gather_kernel, in_specs=[smem, smem, vmem, anyp], out_spec...  19.5 us
    pallas_call x1, Pallas kernels, image_attention(): pl.pallas_call(functools.partial(image_kernel, chunk=256, unit=unit), gri...  18.7 us
    pallas_call x2, Pallas kernels, text_attention(): pl.pallas_call(functools.partial(text_kernel, unit=unit), grid=(heads,),...  12.9 us
    ppermute x1, starting transfers between devices, body(): theirs = lax.ppermute(away, 'seq', [(0, 1), (1, 0)])  2.98 us
    another operation x1, local copies, waits for them, and re-layouts, body(): (ka, va), (kb, vb) = (own, swapped)  2.12 us
  transfers between devices with their start and end apart: 1, of which 0 were waited for; matrix products, arithmetic and copies ran while one was open for 0% of the time, Pallas kernels for 6%

profile of v3, /device:TPU:1, one launch (start us, length us, event | category | flops | bytes accessed | tf_op | source)
XLA Modules:
  0.0 100.4 jit_solution(7123232161324027600)
XLA Ops:
  0.0 1.0 %copy.11 = bf16[1,512,64]{2,1,0:T(8,128)(2,1)S(1)} copy(f32[1,512,64]{1,2,0:T(8,128)} %param.10) | data formatting | bytes 196608 | tf_op args[0]
  1.0 0.7 pad_maximum_fusion.lat_ref
  1.8 19.5 %gather.1 = (bf16[256,128]{1,0:T(8,128)(2,1)}, bf16[256,128]{1,0:T(8,128)(2,1)}, bf16[2,2,128,768]{3,2,1,0:T(8,128)(2,1)}) custom-call(s32[8]{0:T(128)} %anc_ref.5, s32[8]{0:T(128)} %ord_ref.5, bf16[256,128]{1,0:T(8,128)(2,1)} %pad_maximum_fusion.lat_ref, bf16[2,256,768]{2,1,0:T(8,128)(2,1)} %bitcast.18), custom_call_target="tpu_custom_call" | custom-call | bytes 20000000 | tf_op jit(solution)/shard_map/gather/pallas_call | solution.py:234
  21.3 39.9 %project_routed.1 = (bf16[1024,768]{1,0:T(8,128)(2,1)}, bf16[1024,768]{1,0:T(8,128)(2,1)}, bf16[1024,768]{1,0:T(8,128)(2,1)}, bf16[3,2,2,128,768]{4,3,2,1,0:T(8,128)(2,1)}, bf16[2,128,768]{2,1,0:T(8,128)(2,1)}) custom-call(s32[8]{0:T(128)} %anc_ref.5, s32[8]{0:T(128)} %ord_ref.5, bf16[2,2,128,768]{3,2,1,0:T(8,128)(2,1)} %get-tuple-element.17.own_ref, ...), custom_call_target="tpu_custom_call" | custom-call | flops 14495514624 | bytes 18874368 | tf_op jit(solution)/shard_map/project_routed/pallas_call | solution.py:88
  61.2 18.7 %image.1 = (f32[1024,768]{1,0:T(8,128)}, f32[1024,768]{1,0:T(8,128)}, bf16[2,128,768]{2,1,0:T(8,128)(2,1)}, bf16[2,128,768]{2,1,0:T(8,128)(2,1)}) custom-call(s32[8]{0:T(128)} %anc_ref.5, s32[8]{0:T(128)} %ord_ref.5, bf16[2,2,128,768]{3,2,1,0:T(8,128)(2,1)} %get-tuple-element.17.own_ref, bf16[3,2,2,128,768]{4,3,2,1,0:T(8,128)(2,1)} %get-tuple-element.21.others_ref, ...), custom_call_target="tpu_custom_call" | custom-call | flops 6442450944 | bytes 11010048 | tf_op jit(solution)/shard_map/image/pallas_call | solution.py:421
  79.9 2.1 %slice_bitcast_fusion = (bf16[128,768]{1,0:T(8,128)(2,1)}, bf16[128,768]{1,0:T(8,128)(2,1)}, bf16[128,768]{1,0:T(8,128)(2,1)}, bf16[128,768]{1,0:T(8,128)(2,1)}) fusion(bf16[2,128,768]{2,1,0:T(8,128)(2,1)} %get-tuple-element.26, bf16[2,128,768]{2,1,0:T(8,128)(2,1)} %get-tuple-element.25), kind=kLoop, calls=%fused_computation.3 | loop fusion | bytes 1572864 | tf_op jit(solution)/shard_map/unstack | solution.py:451
  82.0 6.5 %text_0.1 = bf16[512,768]{1,0:T(8,128)(2,1)} custom-call(bf16[1024,768]{1,0:T(8,128)(2,1)} %get-tuple-element.20.q_ref, bf16[128,768]{1,0:T(8,128)(2,1)} %get-tuple-element.37.ka_ref, bf16[128,768]{1,0:T(8,128)(2,1)} %get-tuple-element.32.kb_ref, bf16[128,768]{1,0:T(8,128)(2,1)} %get-tuple-element.38.va_ref, bf16[128,768]{1,0:T(8,128)(2,1)} %get-tuple-element.31.vb_ref, ...), custom_call_target="tpu_custom_call" | custom-call | flops 805306368 | bytes 5505024 | tf_op jit(solution)/shard_map/text_0/pallas_call | solution.py:153
  88.5 3.0 %collective-permute-start = (bf16[512,768]{1,0:T(8,128)(2,1)}, bf16[512,768]{1,0:T(8,128)(2,1)S(1)}, u32[]{:S(2)}, u32[]{:S(2)}) collective-permute-start(bf16[512,768]{1,0:T(8,128)(2,1)} %text_0.1), channel_id=1, source_target_pairs={{0,1},{1,0},{2,3},{3,2},{4,5},{5,4},{6,7},{7,6},{8,9},{9,8},{10,11... | collective-permute-start | bytes 2359304 | tf_op jit(solution)/shard_map/ppermute | solution.py:462
  91.5 6.5 %text_1.1 = bf16[512,768]{1,0:T(8,128)(2,1)} custom-call(bf16[1024,768]{1,0:T(8,128)(2,1)} %get-tuple-element.20.q_ref, bf16[128,768]{1,0:T(8,128)(2,1)} %get-tuple-element.37.ka_ref, bf16[128,768]{1,0:T(8,128)(2,1)} %get-tuple-element.32.kb_ref, bf16[128,768]{1,0:T(8,128)(2,1)} %get-tuple-element.38.va_ref, bf16[128,768]{1,0:T(8,128)(2,1)} %get-tuple-element.31.vb_ref, ...), custom_call_target="tpu_custom_call" | custom-call | flops 805306368 | bytes 5505024 | tf_op jit(solution)/shard_map/text_1/pallas_call | solution.py:153
  97.9 0.0 collective-permute-done
  97.9 1.2 %broadcast_select_fusion.1 = (bf16[512,768]{1,0:T(8,128)(2,1)S(1)}, bf16[512,768]{1,0:T(8,128)(2,1)S(1)}) fusion(bf16[512,768]{1,0:T(8,128)(2,1)} %text_1.1, bf16[512,768]{1,0:T(8,128)(2,1)S(1)} %collective-permute-done, pred[]{:T(512)S(6)} %eq.4), kind=kLoop, calls=%fused_computation.2 | loop fusion | flops 786432 | bytes 3145729 | tf_op jit(solution)/shard_map/jit(_where)/select_n | solution.py:464
  99.2 1.3 %maximum_bitcast_fusion = bf16[1,512,1536]{2,1,0:T(8,128)(2,1)} fusion(bf16[512,768]{1,0:T(8,128)(2,1)S(1)} %get-tuple-element.30, bf16[512,768]{1,0:T(8,128)(2,1)S(1)} %get-tuple-element.29), kind=kLoop, calls=%fused_computation | loop fusion | flops 3145728 | bytes 3145728 | tf_op jit(solution)/shard_map/broadcast_in_dim | solution.py:466
  (1 shorter events, 0.0 us)
Async XLA Ops:
  88.5 9.4 %collective-permute-start = (bf16[512,768]{1,0:T(8,128)(2,1)}, bf16[512,768]{1,0:T(8,128)(2,1)S(1)}, u32[]{:S(2)}, u32[]{:S(2)}) collective-permute-start(bf16[512,768]{1,0:T(8,128)(2,1)} %text_0.1), channel_id=1, source_target_pairs={{0,1},{1,0},{2,3},{3,2},{4,5},{5,4},{6,7},{7,6},{8,9},{9,8},{10,11... | collective-permute-start | bytes 2359304 | tf_op jit(solution)/shard_map/ppermute | solution.py:462
